TPU v7x, 256 devices: a whole 4x4x8 slice. The times are simulated.
256 devices in a mesh: sample: 16 (over z_hi, y, core), space: 16 (over x, z_lo).
Axes of the slice: x: 4, y: 4, z: 8 (z_hi: 2, z_lo: 4; z = z_hi * 4 + z_lo), core: 2. Of those that a mesh axis runs over, the one named last changes fastest.
Arguments:
- volume: bfloat16 [16, 4, 16, 8, 128], P('sample', None, 'space'), may hold values from -6 to 6
- cotangent: bfloat16 [16, 128, 16, 8, 128], P('sample', None, 'space'), may hold values from -6 to 6
- weight_one: bfloat16 [3, 3, 3, 4, 32], replicated, may hold values from -0.625 to 0.625
- bias_one: float32 [32], replicated, may hold values from -0.5 to 0.5
- weight_two: bfloat16 [3, 3, 3, 32, 64], replicated, may hold values from -0.21875 to 0.21875
- bias_two: float32 [64], replicated, may hold values from -0.5 to 0.5
- weight_three: bfloat16 [3, 3, 3, 64, 128], replicated, may hold values from -0.15625 to 0.15625
- bias_three: float32 [128], replicated, may hold values from -0.5 to 0.5
Outputs:
- grad_weight_one: float32 [3, 3, 3, 4, 32], replicated
- grad_bias_one: float32 [32], replicated
- grad_weight_two: float32 [3, 3, 3, 32, 64], replicated
- grad_bias_two: float32 [64], replicated
- grad_weight_three: float32 [3, 3, 3, 64, 128], replicated
- grad_bias_three: float32 [128], replicated
All inputs are finite; a program needn't handle non-finite values.
Results may differ from a plain program's by a relative error of at most 0.015.
Values may be sent and summed in bfloat16 or wider, within the bound.
A program may use at most 64 MiB of HBM per device.

v0:
```python
import math

import jax
import jax.numpy as jnp
from jax import lax
from jax.sharding import PartitionSpec as P

negative_slope = 0.3


def with_halo(array, sides, width):
    for axis, dim in sides:
        size, length = (lax.axis_size(axis), array.shape[dim])
        up = [(i, (i + 1) % size) for i in range(size - 1)]
        down = [(j, i) for i, j in up]
        last = lax.slice_in_dim(array, length - width, length, axis=dim)
        leading = lax.slice_in_dim(array, 0, width, axis=dim)
        before = lax.ppermute(last, axis, up)
        after = lax.ppermute(leading, axis, down)
        array = jnp.concatenate([before, array, after], axis=dim)
    return array


def leaky(pre):
    return negative_slope * pre + (1.0 - negative_slope) * jax.nn.softplus(pre)


def slope_of(pre):
    return negative_slope + (1.0 - negative_slope) * jax.nn.sigmoid(pre)


def all_windows(padded):
    channels = padded.shape[0]
    size_x = padded.shape[1] - 2
    size_y = padded.shape[2] - 2
    size_z = padded.shape[3] - 2
    pieces = []
    for along_x in range(3):
        for along_y in range(3):
            for along_z in range(3):
                pieces.append(
                    padded[
                        :,
                        along_x : along_x + size_x,
                        along_y : along_y + size_y,
                        along_z : along_z + size_z,
                    ].reshape(channels, -1)
                )
    return jnp.concatenate(pieces, axis=0)


def conv_taps(padded, weight):
    channels = padded.shape[0]
    size_x = padded.shape[1] - 2
    size_y = padded.shape[2] - 2
    size_z = padded.shape[3] - 2
    total = jnp.zeros((weight.shape[4], size_x * size_y * size_z), jnp.float32)
    for along_x in range(3):
        for along_y in range(3):
            for along_z in range(3):
                window = padded[
                    :,
                    along_x : along_x + size_x,
                    along_y : along_y + size_y,
                    along_z : along_z + size_z,
                ].reshape(channels, -1)
                total = total + lax.dot_general(
                    weight[along_x, along_y, along_z],
                    window,
                    (((0,), (0,)), ((), ())),
                    preferred_element_type=jnp.float32,
                )
    return total


def transpose_taps(padded, weight):
    channels = padded.shape[0]
    size_x = padded.shape[1] - 2
    size_y = padded.shape[2] - 2
    size_z = padded.shape[3] - 2
    total = jnp.zeros((weight.shape[3], size_x * size_y * size_z), jnp.float32)
    for along_x in range(3):
        for along_y in range(3):
            for along_z in range(3):
                start_x = 2 - along_x
                start_y = 2 - along_y
                start_z = 2 - along_z
                window = padded[
                    :,
                    start_x : start_x + size_x,
                    start_y : start_y + size_y,
                    start_z : start_z + size_z,
                ].reshape(channels, -1)
                total = total + lax.dot_general(
                    weight[along_x, along_y, along_z],
                    window,
                    (((1,), (0,)), ((), ())),
                    preferred_element_type=jnp.float32,
                )
    return total


def weight_taps(padded, delta):
    channels = padded.shape[0]
    size_x = padded.shape[1] - 2
    size_y = padded.shape[2] - 2
    size_z = padded.shape[3] - 2
    pieces = []
    for along_x in range(3):
        for along_y in range(3):
            for along_z in range(3):
                window = padded[
                    :,
                    along_x : along_x + size_x,
                    along_y : along_y + size_y,
                    along_z : along_z + size_z,
                ].reshape(channels, -1)
                pieces.append(
                    lax.dot_general(
                        window, delta, (((1,), (1,)), ((), ())), preferred_element_type=jnp.float32
                    )
                )
    return jnp.stack(pieces).reshape(3, 3, 3, channels, delta.shape[0])


def pad_forward(field):
    widened = with_halo(field, (("space", 1),), 1)
    return jnp.pad(widened, ((0, 0), (0, 0), (1, 1), (1, 1)))


def pad_backward(field):
    widened = with_halo(field, (("space", 1),), 1)
    return jnp.pad(widened, ((0, 0), (0, 0), (1, 1), (1, 1)))


def local(volume, cotangent, weight_one, bias_one, weight_two, bias_two, weight_three, bias_three):
    fields = volume[0]
    grid = fields.shape[1:]
    cells = grid[0] * grid[1] * grid[2]
    scale = 1.0 / math.sqrt(lax.axis_size("sample") * lax.axis_size("space") * cells)
    inputs_one = weight_one.shape[3]
    width_one = weight_one.shape[4]
    width_two = weight_two.shape[4]
    width_three = weight_three.shape[4]
    padded_zero = pad_forward(fields)
    stacked_zero = all_windows(padded_zero)
    flat_one = weight_one.reshape(27 * inputs_one, width_one)
    pre_one = (
        lax.dot_general(
            flat_one, stacked_zero, (((0,), (0,)), ((), ())), preferred_element_type=jnp.float32
        )
        + bias_one[:, None]
    )
    act_one = leaky(pre_one).astype(jnp.bfloat16).reshape((width_one,) + grid)
    padded_one = pad_forward(act_one)
    pre_two = conv_taps(padded_one, weight_two) + bias_two[:, None]
    act_two = leaky(pre_two).astype(jnp.bfloat16).reshape((width_two,) + grid)
    padded_two = pad_forward(act_two)
    pre_three = conv_taps(padded_two, weight_three) + bias_three[:, None]
    upstream_rows = cotangent[0].reshape(width_three, -1).astype(jnp.float32)
    delta_three = (upstream_rows * scale * slope_of(pre_three)).astype(jnp.bfloat16)
    back_three = pad_backward(delta_three.reshape((width_three,) + grid))
    grad_weight_three = weight_taps(padded_two, delta_three)
    grad_bias_three = jnp.sum(delta_three.astype(jnp.float32), axis=1)
    flow_two = transpose_taps(back_three, weight_three)
    delta_two = (flow_two * slope_of(pre_two)).astype(jnp.bfloat16)
    back_two = pad_backward(delta_two.reshape((width_two,) + grid))
    grad_weight_two = weight_taps(padded_one, delta_two)
    grad_bias_two = jnp.sum(delta_two.astype(jnp.float32), axis=1)
    flow_one = transpose_taps(back_two, weight_two)
    delta_one = (flow_one * slope_of(pre_one)).astype(jnp.bfloat16)
    grad_weight_one = lax.dot_general(
        stacked_zero, delta_one, (((1,), (1,)), ((), ())), preferred_element_type=jnp.float32
    ).reshape(3, 3, 3, inputs_one, width_one)
    grad_bias_one = jnp.sum(delta_one.astype(jnp.float32), axis=1)
    grads = (
        grad_weight_one,
        grad_bias_one,
        grad_weight_two,
        grad_bias_two,
        grad_weight_three,
        grad_bias_three,
    )
    totals = lax.psum(
        (grads[0], grads[1], grads[2], grads[3], grads[4], grads[5]), ("sample", "space")
    )
    return (totals[0], totals[1], totals[2], totals[3], totals[4], totals[5])


def solution(mesh):
    placed = (
        P("sample", None, "space", None, None),
        P("sample", None, "space", None, None),
        P(),
        P(),
        P(),
        P(),
        P(),
        P(),
    )
    return jax.shard_map(
        local, mesh=mesh, in_specs=placed, out_specs=(P(), P(), P(), P(), P(), P()), check_vma=False
    )
```

profile of v0, /device:TPU:1, one launch (start us, length us, event | category | flops | bytes accessed | tf_op | source)
XLA Modules:
  0.0 368.6 jit_solution(1059301853339657724)
XLA Ops:
  7.2 1.3 collective-permute-start.1
  8.5 5.0 %collective-permute-start = (bf16[4,1,8,128]{3,2,0,1:T(8,128)(2,1)}, bf16[4,1,8,128]{3,2,0,1:T(8,128)(2,1)S(1)}, u32[]{:S(2)}, u32[]{:S(2)}) collective-permute-start(bf16[4,1,8,128]{3,2,0,1:T(8,128)(2,1)} %bitcast.1742), channel_id=1, source_target_pairs={{0,1},{1,2},{2,3},{3,4},{4,5},{5,6},{6,7},{7,8},{8,9},{9,10},{10,1... | collective-permute-start | bytes 24584 | tf_op jit(solution)/shard_map/ppermute | solution.py:18
  13.5 0.7 copy.681
  14.2 0.8 reshape.525
  15.0 0.8 select_maximum_fusion.6
  16.2 0.4 concatenate.19
  16.6 1.6 fusion.148
  18.2 1.3 collective-permute-start.3
  19.5 4.2 %collective-permute-start.2 = (bf16[32,1,8,128]{3,2,0,1:T(8,128)(2,1)S(1)}, bf16[32,1,8,128]{3,2,0,1:T(8,128)(2,1)S(1)}, u32[]{:S(2)}, u32[]{:S(2)}) collective-permute-start(bf16[32,1,8,128]{3,2,0,1:T(8,128)(2,1)S(1)} %bitcast.1735), channel_id=1, source_target_pairs={{0,1},{1,2},{2,3},{3,4},{4,5},{5,6},{6,7},{7,8},{8,9},{9,10},{10,1... | collective-permute-start | bytes 196616 | tf_op jit(solution)/shard_map/ppermute | solution.py:18
  23.7 1.3 collective-permute-done.2
  25.0 0.6 select_maximum_fusion.4
  25.7 0.4 fusion.642
  26.2 0.3 copy-done.2
  31.4 0.3 fusion.57
  32.6 1.1 fusion.142
  33.7 1.3 collective-permute-start.5
  35.0 4.3 %collective-permute-start.4 = (bf16[64,1,8,128]{3,2,0,1:T(8,128)(2,1)S(1)}, bf16[64,1,8,128]{3,2,0,1:T(8,128)(2,1)S(1)}, u32[]{:S(2)}, u32[]{:S(2)}) collective-permute-start(bf16[64,1,8,128]{3,2,0,1:T(8,128)(2,1)S(1)} %bitcast.1727), channel_id=1, source_target_pairs={{0,1},{1,2},{2,3},{3,4},{4,5},{5,6},{6,7},{7,8},{8,9},{9,10},{10,1... | collective-permute-start | bytes 393224 | tf_op jit(solution)/shard_map/ppermute | solution.py:18
  39.4 1.0 copy.16
  40.5 0.8 collective-permute-done.4
  41.3 1.1 fusion.13
  42.6 0.8 fusion.638
  43.9 0.3 fusion.255
  44.1 0.3 convolution_add_fusion.14
  44.4 0.3 convolution_add_fusion.13
  44.7 0.3 convolution_add_fusion.12
  44.9 0.3 fusion.28
  45.2 0.3 convolution_add_fusion.10
  45.5 0.3 convolution_add_fusion.9
  45.8 0.3 convolution_add_fusion.8
  46.0 0.3 convolution_add_fusion.7
  46.3 0.3 convolution_add_fusion.6
  46.5 0.3 convolution_add_fusion.5
  46.8 0.3 convolution_add_fusion.4
  47.1 0.3 convolution_add_fusion.3
  47.3 0.3 convolution_add_fusion.2
  47.6 0.3 convolution_add_fusion.1
  47.9 0.3 fusion.27
  48.1 0.3 fusion.26
  48.4 0.3 fusion.25
  48.7 0.3 fusion.24
  48.9 0.3 fusion.23
  49.2 0.3 fusion.22
  49.5 0.3 fusion.21
  49.8 0.3 fusion.20
  50.3 0.3 fusion.18
  50.8 0.4 convert_reduce_fusion
  51.2 1.3 collective-permute-start.7
  52.5 6.7 %collective-permute-start.6 = (bf16[128,1,8,128]{0,3,2,1:T(8,128)(2,1)S(1)}, bf16[128,1,8,128]{0,3,2,1:T(8,128)(2,1)S(1)}, u32[]{:S(2)}, u32[]{:S(2)}) collective-permute-start(bf16[128,1,8,128]{0,3,2,1:T(8,128)(2,1)S(1)} %bitcast.1565), channel_id=1, source_target_pairs={{0,1},{1,2},{2,3},{3,4},{4,5},{5,6},{6,7},{7,8},{8,9},{9,10},{10,1... | collective-permute-start | bytes 786440 | tf_op jit(solution)/shard_map/ppermute | solution.py:18
  64.2 0.3 select_maximum_fusion.2
  64.4 0.3 fusion.641
  64.7 0.3 copy-done.1
  65.0 0.9 fusion.640
  71.7 0.3 convert_reduce_fusion.1
  72.0 1.3 collective-permute-start.9
  73.3 6.7 %collective-permute-start.8 = (bf16[64,1,8,128]{3,2,0,1:T(8,128)(2,1)S(1)}, bf16[64,1,8,128]{3,2,0,1:T(8,128)(2,1)S(1)}, u32[]{:S(2)}, u32[]{:S(2)}) collective-permute-start(bf16[64,1,8,128]{3,2,0,1:T(8,128)(2,1)S(1)} %bitcast.1724), channel_id=1, source_target_pairs={{0,1},{1,2},{2,3},{3,4},{4,5},{5,6},{6,7},{7,8},{8,9},{9,10},{10,1... | collective-permute-start | bytes 393224 | tf_op jit(solution)/shard_map/ppermute | solution.py:18
  84.5 0.8 copy-done.22
  85.4 1.1 select_maximum_fusion
  86.5 0.3 fusion.637
  86.8 0.8 fusion.636
  91.6 0.3 convert_reduce_fusion.2
  92.1 92.9 %all-reduce.5 = (f32[3,3,3,4,32]{4,3,2,1,0:T(4,128)}, f32[32]{0:T(128)}, f32[64]{0:T(128)}, f32[128]{0:T(128)}) all-reduce(f32[3,3,3,4,32]{4,3,2,1,0:T(4,128)S(1)} %reshape.634, f32[32]{0:T(128)S(1)} %get-tuple-element.136, f32[64]{0:T(128)S(1)} %get-tuple-element.138, ...), channel_id=1, replica_groups=mesh['sample'=16,'space'=16] {'sample','space'}, use_global_device_ids=true, to_apply=%region_0.1 | all-reduce | flops 3680 | bytes 29440 | tf_op jit(solution)/shard_map/psum | solution.py:184
  185.0 172.8 %all-reduce.9.cloned.1.call-done = (f32[3,3,3,32,64]{4,3,2,1,0:T(8,128)}, f32[3,3,3,64,128]{4,3,2,1,0:T(8,128)}) async-done(((f32[3,3,3,32,64]{4,3,2,1,0:T(8,128)}, f32[3,3,3,64,128]{4,3,2,1,0:T(8,128)}), (f32[3,3,3,32,64]{4,3,2,1,0:T(8,128)}, f32[3,3,3,64,128]{4,3,2,1,0:T(8,128)})) %all-reduce.9.cloned.1.call-update) | async-done | bytes 1105936 | tf_op jit(solution)/shard_map/psum | solution.py:184
  357.7 1.8 copy.737
  359.5 2.2 copy.738
  (224 shorter events, 26.2 us)
Async XLA Ops:
  7.2 350.6 %all-reduce.9.cloned.1.call-start = ((), (), s32[]{:S(2)}) async-start(), calls=%async_computation | async-start | bytes 2654208 | tf_op jit(solution)/shard_map/psum | solution.py:184
  7.2 7.8 %collective-permute-start.1 = (bf16[4,1,8,128]{3,2,0,1:T(8,128)(2,1)}, bf16[4,1,8,128]{3,2,0,1:T(8,128)(2,1)S(1)}, u32[]{:S(2)}, u32[]{:S(2)}) collective-permute-start(bf16[4,1,8,128]{3,2,0,1:T(8,128)(2,1)} %bitcast.1741), channel_id=1, source_target_pairs={{1,0},{2,1},{3,2},{4,3},{5,4},{6,5},{7,6},{8,7},{9,8},{10,9},{11,1... | collective-permute-start | bytes 24584 | tf_op jit(solution)/shard_map/ppermute | solution.py:19
  8.5 6.5 %collective-permute-start = (bf16[4,1,8,128]{3,2,0,1:T(8,128)(2,1)}, bf16[4,1,8,128]{3,2,0,1:T(8,128)(2,1)S(1)}, u32[]{:S(2)}, u32[]{:S(2)}) collective-permute-start(bf16[4,1,8,128]{3,2,0,1:T(8,128)(2,1)} %bitcast.1742), channel_id=1, source_target_pairs={{0,1},{1,2},{2,3},{3,4},{4,5},{5,6},{6,7},{7,8},{8,9},{9,10},{10,1... | collective-permute-start | bytes 24584 | tf_op jit(solution)/shard_map/ppermute | solution.py:18
  18.2 5.5 %collective-permute-start.3 = (bf16[32,1,8,128]{3,2,0,1:T(8,128)(2,1)S(1)}, bf16[32,1,8,128]{3,2,0,1:T(8,128)(2,1)S(1)}, u32[]{:S(2)}, u32[]{:S(2)}) collective-permute-start(bf16[32,1,8,128]{3,2,0,1:T(8,128)(2,1)S(1)} %bitcast.1734), channel_id=1, source_target_pairs={{1,0},{2,1},{3,2},{4,3},{5,4},{6,5},{7,6},{8,7},{9,8},{10,9},{11,1... | collective-permute-start | bytes 196616 | tf_op jit(solution)/shard_map/ppermute | solution.py:19
  19.5 5.5 %collective-permute-start.2 = (bf16[32,1,8,128]{3,2,0,1:T(8,128)(2,1)S(1)}, bf16[32,1,8,128]{3,2,0,1:T(8,128)(2,1)S(1)}, u32[]{:S(2)}, u32[]{:S(2)}) collective-permute-start(bf16[32,1,8,128]{3,2,0,1:T(8,128)(2,1)S(1)} %bitcast.1735), channel_id=1, source_target_pairs={{0,1},{1,2},{2,3},{3,4},{4,5},{5,6},{6,7},{7,8},{8,9},{9,10},{10,1... | collective-permute-start | bytes 196616 | tf_op jit(solution)/shard_map/ppermute | solution.py:18
  23.7 8.0 %copy-start.11 = (bf16[32,1,8,128]{3,2,0,1:T(8,128)(2,1)}, bf16[32,1,8,128]{3,2,0,1:T(8,128)(2,1)S(1)}, u32[]{:S(2)}) copy-start(bf16[32,1,8,128]{3,2,0,1:T(8,128)(2,1)S(1)} %collective-permute-done.3) | copy-start | bytes 196612
  25.0 2.7 copy-start.13
  25.5 0.9 copy-start.2
  25.7 1.2 copy-start.7
  25.7 1.2 copy-start.9
  26.1 4.3 %copy-start.3 = (bf16[32,1,8,128]{3,2,0,1:T(8,128)(2,1)}, bf16[32,1,8,128]{3,2,0,1:T(8,128)(2,1)S(1)}, u32[]{:S(2)}) copy-start(bf16[32,1,8,128]{3,2,0,1:T(8,128)(2,1)S(1)} %get-tuple-element.91) | copy-start | bytes 196612
  26.1 4.5 %copy-start.5 = (bf16[32,1,8,128]{3,2,0,1:T(8,128)(2,1)}, bf16[32,1,8,128]{3,2,0,1:T(8,128)(2,1)S(1)}, u32[]{:S(2)}) copy-start(bf16[32,1,8,128]{3,2,0,1:T(8,128)(2,1)S(1)} %get-tuple-element.92) | copy-start | bytes 196612
  26.1 5.2 %copy-start.15 = (bf16[32,1,8,128]{3,2,0,1:T(8,128)(2,1)}, bf16[32,1,8,128]{3,2,0,1:T(8,128)(2,1)S(1)}, u32[]{:S(2)}) copy-start(bf16[32,1,8,128]{3,2,0,1:T(8,128)(2,1)S(1)} %get-tuple-element.93) | copy-start | bytes 196612
  26.2 6.5 %copy-start.24 = (bf16[32,1,8,128]{3,2,0,1:T(8,128)(2,1)}, bf16[32,1,8,128]{3,2,0,1:T(8,128)(2,1)S(1)}, u32[]{:S(2)}) copy-start(bf16[32,1,8,128]{3,2,0,1:T(8,128)(2,1)S(1)} %get-tuple-element.84) | copy-start | bytes 196612
  31.7 1.0 copy-start.26
  31.9 7.5 %copy-start.23 = (bf16[1,128,1,8,128]{4,3,2,1,0:T(8,128)(2,1)S(1)}, bf16[1,128,1,8,128]{4,3,2,1,0:T(8,128)(2,1)}, u32[]{:S(2)}) copy-start(bf16[1,128,1,8,128]{4,3,2,1,0:T(8,128)(2,1)} %param.9) | copy-start | bytes 786436
  33.7 6.7 %collective-permute-start.5 = (bf16[64,1,8,128]{3,2,0,1:T(8,128)(2,1)S(1)}, bf16[64,1,8,128]{3,2,0,1:T(8,128)(2,1)S(1)}, u32[]{:S(2)}, u32[]{:S(2)}) collective-permute-start(bf16[64,1,8,128]{3,2,0,1:T(8,128)(2,1)S(1)} %bitcast.1726), channel_id=1, source_target_pairs={{1,0},{2,1},{3,2},{4,3},{5,4},{6,5},{7,6},{8,7},{9,8},{10,9},{11,1... | collective-permute-start | bytes 393224 | tf_op jit(solution)/shard_map/ppermute | solution.py:19
  35.0 6.3 %collective-permute-start.4 = (bf16[64,1,8,128]{3,2,0,1:T(8,128)(2,1)S(1)}, bf16[64,1,8,128]{3,2,0,1:T(8,128)(2,1)S(1)}, u32[]{:S(2)}, u32[]{:S(2)}) collective-permute-start(bf16[64,1,8,128]{3,2,0,1:T(8,128)(2,1)S(1)} %bitcast.1727), channel_id=1, source_target_pairs={{0,1},{1,2},{2,3},{3,4},{4,5},{5,6},{6,7},{7,8},{8,9},{9,10},{10,1... | collective-permute-start | bytes 393224 | tf_op jit(solution)/shard_map/ppermute | solution.py:18
  42.6 1.0 copy-start
  49.7 1.0 copy-start.17
  49.8 1.0 copy-start.27
  51.2 12.9 %collective-permute-start.7 = (bf16[128,1,8,128]{0,3,2,1:T(8,128)(2,1)S(1)}, bf16[128,1,8,128]{0,3,2,1:T(8,128)(2,1)S(1)}, u32[]{:S(2)}, u32[]{:S(2)}) collective-permute-start(bf16[128,1,8,128]{0,3,2,1:T(8,128)(2,1)S(1)} %bitcast.1564), channel_id=1, source_target_pairs={{1,0},{2,1},{3,2},{4,3},{5,4},{6,5},{7,6},{8,7},{9,8},{10,9},{11,1... | collective-permute-start | bytes 786440 | tf_op jit(solution)/shard_map/ppermute | solution.py:19
  52.5 11.7 %collective-permute-start.6 = (bf16[128,1,8,128]{0,3,2,1:T(8,128)(2,1)S(1)}, bf16[128,1,8,128]{0,3,2,1:T(8,128)(2,1)S(1)}, u32[]{:S(2)}, u32[]{:S(2)}) collective-permute-start(bf16[128,1,8,128]{0,3,2,1:T(8,128)(2,1)S(1)} %bitcast.1565), channel_id=1, source_target_pairs={{0,1},{1,2},{2,3},{3,4},{4,5},{5,6},{6,7},{7,8},{8,9},{9,10},{10,1... | collective-permute-start | bytes 786440 | tf_op jit(solution)/shard_map/ppermute | solution.py:18
  64.1 0.9 copy-start.1
  70.7 1.0 copy-start.29
  71.2 8.8 %copy-start.10 = (bf16[32,1,8,128]{3,2,0,1:T(8,128)(2,1)S(1)}, bf16[32,1,8,128]{3,2,0,1:T(8,128)(2,1)}, u32[]{:S(2)}) copy-start(bf16[32,1,8,128]{3,2,0,1:T(8,128)(2,1)} %copy-done.9) | copy-start | bytes 196612
  71.4 9.3 %copy-start.14 = (bf16[32,1,8,128]{3,2,0,1:T(8,128)(2,1)S(1)}, bf16[32,1,8,128]{3,2,0,1:T(8,128)(2,1)}, u32[]{:S(2)}) copy-start(bf16[32,1,8,128]{3,2,0,1:T(8,128)(2,1)} %copy-done.13) | copy-start | bytes 196612
  71.6 9.2 %copy-start.8 = (bf16[32,1,8,128]{3,2,0,1:T(8,128)(2,1)S(1)}, bf16[32,1,8,128]{3,2,0,1:T(8,128)(2,1)}, u32[]{:S(2)}) copy-start(bf16[32,1,8,128]{3,2,0,1:T(8,128)(2,1)} %copy-done.7) | copy-start | bytes 196612
  72.0 13.3 %collective-permute-start.9 = (bf16[64,1,8,128]{3,2,0,1:T(8,128)(2,1)S(1)}, bf16[64,1,8,128]{3,2,0,1:T(8,128)(2,1)S(1)}, u32[]{:S(2)}, u32[]{:S(2)}) collective-permute-start(bf16[64,1,8,128]{3,2,0,1:T(8,128)(2,1)S(1)} %bitcast.1723), channel_id=1, source_target_pairs={{1,0},{2,1},{3,2},{4,3},{5,4},{6,5},{7,6},{8,7},{9,8},{10,9},{11,1... | collective-permute-start | bytes 393224 | tf_op jit(solution)/shard_map/ppermute | solution.py:19
  73.3 12.1 %collective-permute-start.8 = (bf16[64,1,8,128]{3,2,0,1:T(8,128)(2,1)S(1)}, bf16[64,1,8,128]{3,2,0,1:T(8,128)(2,1)S(1)}, u32[]{:S(2)}, u32[]{:S(2)}) collective-permute-start(bf16[64,1,8,128]{3,2,0,1:T(8,128)(2,1)S(1)} %bitcast.1724), channel_id=1, source_target_pairs={{0,1},{1,2},{2,3},{3,4},{4,5},{5,6},{6,7},{7,8},{8,9},{9,10},{10,1... | collective-permute-start | bytes 393224 | tf_op jit(solution)/shard_map/ppermute | solution.py:18
  80.2 2.5 copy-start.16
  80.3 2.5 copy-start.6
  80.5 2.5 copy-start.4
  81.2 2.5 copy-start.12
  81.8 2.5 copy-start.25
  84.5 0.8 copy-start.22
  85.4 1.1 copy-start.20
  85.4 1.1 copy-start.18
  87.5 0.9 copy-start.21
  89.8 1.2 copy-start.19
  90.4 1.2 copy-start.28
Sparse Core Ops, SparseCore 0:
  85.5 272.2 all-reduce.8
where the time goes:
time: 369 us
  waiting for transfers between devices  175 us (47%)
  blocking collectives  92.9 us (25%)
  matrix products  34.7 us (9%)
  starting transfers between devices  33.4 us (9%)
  between operations  15.5 us (4%)
  local copies, waits for them, and re-layouts  13.2 us (4%)
  other arithmetic  3.83 us (1%)
    psum x1, waiting for transfers between devices, local(): lax.psum((grads[0], grads[1], grads[2], grads[3], grads[4], grads[5]), ('...  173 us
    psum x1, blocking collectives, local(): lax.psum((grads[0], grads[1], grads[2], grads[3], grads[4], grads[5]), ('...  92.9 us
    ppermute x5, starting transfers between devices, with_halo(): before = lax.ppermute(last, axis, up)  26.9 us
    dot_general x54, matrix products, conv_taps(): lax.dot_general(weight[along_x, along_y, along_z], window, (((0,), (0,)),...  14.1 us
    dot_general x54, matrix products, transpose_taps(): lax.dot_general(weight[along_x, along_y, along_z], window, (((1,), (0,)),...  9.68 us
    dot_general x54, matrix products, weight_taps(): lax.dot_general(window, delta, (((1,), (1,)), ((), ())), preferred_elemen...  9.19 us
  transfers between devices with their start and end apart: 11, of which 3 were waited for; matrix products, arithmetic and copies ran while one was open for 5% of the time, Pallas kernels for 0%

commit v1 on v0

v1 whole, which is shorter than its diff:
```python
import math

import jax
import jax.numpy as jnp
from jax import lax
from jax.experimental import pallas as pl
from jax.experimental.pallas import tpu as pltpu
from jax.sharding import PartitionSpec as P

MESH = pl.DeviceIdType.MESH
BF = jnp.bfloat16
F32 = jnp.float32

C0, C1, C2, C3 = 4, 32, 64, 128
YS, ZS, NX = 8, 128, 16
CELLS = YS * ZS
SCALE = 1.0 / math.sqrt(16 * NX * YS * ZS)
NT = (((1,), (1,)), ((), ()))


def home(zh, y, c, q):
    x, k = q // 4, q % 4
    return zh * 8 + y * 2 + k % 2, x * 4 + 2 * c + (k // 2 + x) % 2


def softplus_sigmoid(u):
    e = jnp.exp(-jnp.abs(u))
    return jnp.maximum(u, 0.0) + jnp.log(1.0 + e), e


def leaky(u):
    soft, e = softplus_sigmoid(u)
    return 0.3 * u + 0.7 * soft, e


def slope_from(u, e):
    r = 1.0 / (1.0 + e)
    return 0.3 + 0.7 * jnp.where(u >= 0.0, r, e * r)


def shifted(slab, lane):
    lo = jnp.where(lane == 0, 0.0, pltpu.roll(slab, 1, 1))
    hi = jnp.where(lane == ZS - 1, 0.0, pltpu.roll(slab, ZS - 1, 1))
    return lo.astype(BF), slab.astype(BF), hi.astype(BF)


def spread(ref, base, slab, ysrc, lane):
    width = slab.shape[0]
    parts = shifted(slab, lane)
    for ky in range(3):
        yo = ysrc + 1 - ky
        if 0 <= yo < YS:
            for kz in range(3):
                row = base + (ky * 3 + kz) * width
                ref[row : row + width, yo * ZS : (yo + 1) * ZS] = parts[kz]


def zero_edges(ref, base, width):
    for ky, yo in ((0, 0), (2, YS - 1)):
        row = base + ky * 3 * width
        ref[row : row + 3 * width, yo * ZS : (yo + 1) * ZS] = jnp.zeros((3 * width, ZS), BF)


def body(
    vol, cot, w1, b1, w2, b2, w3, b3,
    o1, ob1, o2, ob2, o3, ob3,
    vols, cotv, cotf, volf, w1f, w1big, w2big, w3t, w3b, w2b, bcols,
    s1, q1, q2, r3, r2, pre, d3, d2, d1, sl1, sl2, fl, tx2, rx2, tx1, rx1,
    acc_a, rx_a0, sum_a, rx_a1, z_a, gath_a,
    g2, acc_b, rx_b0, sum_b, rx_b1, z_b, gath_b,
    g1, acc_c, rx_c0, x_c, z_c,
    vs, vr, cs, cr, fs, fr, a_s, a_r, b_s, b_r, c_s, c_r,
):
    me_s, me_p = lax.axis_index("sample"), lax.axis_index("space")
    zh, y, c = me_s // 8, (me_s // 2) % 4, me_s % 2
    x, zl = me_p // 4, me_p % 4
    q = 4 * x + 2 * ((zl + x) % 2) + c
    work_c = zl // 2
    work_s = zh * 8 + y * 2 + work_c

    rank = x * 4 + y
    zi = zh * 4 + zl
    partner = (me_s + 1 - 2 * c, me_p)

    def xy_peer(d):
        r = (rank + d) % 16
        return r, (zh * 8 + (r % 4) * 2 + c, (r // 4) * 4 + zl)

    def z_peer(d):
        z = (zi + d) % 8
        return ((z // 4) * 8 + y * 2 + c, x * 4 + z % 4)

    sources = []
    targets = []
    for j in range(-3, 4):
        src = q + j
        ok = (src >= 0) & (src < NX)
        sources.append((j, ok, (work_s, src), ok & ((work_s != me_s) | (src != me_p))))
        t = me_p + j
        okt = (t >= 0) & (t < NX)
        ts, tp = home(zh, y, c, t)
        away = (ts != me_s) | (tp != me_p)
        targets.append((j, okt & away, okt & jnp.logical_not(away), (ts, tp)))

    barrier = pltpu.get_barrier_semaphore()
    count = jnp.int32(15 + 7 + 1)
    for d in range(4, 8):
        pl.semaphore_signal(barrier, 1, device_id=z_peer(d), device_id_type=MESH)
    for j, ok, dev, away in sources:
        @pl.when(away)
        def _():
            pl.semaphore_signal(barrier, 1, device_id=dev, device_id_type=MESH)
    for j, remote, local, dev in targets:
        count = count + remote.astype(jnp.int32)
    for d in range(1, 16):
        pl.semaphore_signal(barrier, 1, device_id=xy_peer(d)[1], device_id_type=MESH)
    for d in range(1, 4):
        pl.semaphore_signal(barrier, 1, device_id=z_peer(d), device_id_type=MESH)
    pl.semaphore_signal(barrier, 1, device_id=partner, device_id_type=MESH)

    lane = lax.broadcasted_iota(jnp.int32, (1, ZS), 1)

    w1f[...] = jnp.zeros_like(w1f)
    for kx in range(3):
        for ky in range(3):
            for kz in range(3):
                row = (ky * 3 + kz) * 32 + kx * 4
                w1f[row : row + 4, 0:C1] = w1[kx, ky, kz].astype(F32)
    t1 = w1f[...].T[0:C1]
    for xo in range(5):
        w1big[xo * C1 : (xo + 1) * C1, :] = (pltpu.roll(t1, 4 * xo, 1) if xo else t1).astype(BF)
    bcols[...] = jnp.zeros_like(bcols)
    bcols[:, 0:C1] = jnp.broadcast_to(b1[...].reshape(1, C1), (ZS, C1))
    bcols[:, C2 : 2 * C2] = jnp.broadcast_to(b2[...].reshape(1, C2), (ZS, C2))
    bt = bcols[...].T
    bcols[...] = bt
    b3col = jnp.broadcast_to(b3[...].reshape(1, C3), (ZS, C3)).T
    s1[288:320, :] = jnp.ones((32, CELLS), BF)
    s1[320:384, :] = jnp.zeros((64, CELLS), BF)
    zero_edges(s1, 0, 32)
    for xo in range(5):
        zero_edges(q1, xo * 288, C1)
    q1[1440:1536, :] = jnp.zeros((96, CELLS), BF)
    for xo in range(3):
        zero_edges(q2, xo * 576, C2)
    q2[1728:1744, :] = jnp.ones((16, CELLS), BF)
    q2[1744:1792, :] = jnp.zeros((48, CELLS), BF)
    zero_edges(r3, 0, C3)
    zero_edges(r2, 0, C2)
    r2[576:640, :] = jnp.zeros((64, CELLS), BF)
    volf[224:256, :] = jnp.zeros((32, ZS), F32)
    acc_a[1744:2048, :] = jnp.zeros((304, ZS), BF)

    pl.semaphore_wait(barrier, count)

    def vol_copy(j, dev):
        return pltpu.make_async_remote_copy(
            src_ref=vol.at[0, :, 0], dst_ref=vols.at[3 - j], send_sem=vs.at[3 - j], recv_sem=vr.at[3 - j],
            device_id=dev, device_id_type=MESH)

    for j, remote, local, dev in targets:
        pl.when(remote)(vol_copy(j, dev).start)
        pl.when(local)(pltpu.make_async_copy(vol.at[0, :, 0], vols.at[3 - j], vr.at[3 - j]).start)
    _, cot_remote, cot_local, cot_dev = targets[3]
    cot_out = pltpu.make_async_remote_copy(
        src_ref=cot.at[0, :, 0], dst_ref=cotv, send_sem=cs, recv_sem=cr, device_id=cot_dev, device_id_type=MESH)
    pl.when(cot_remote)(cot_out.start)
    pl.when(cot_local)(pltpu.make_async_copy(cot.at[0, :, 0], cotv, cr).start)

    t2 = jnp.concatenate([w2[...].reshape(864, C2).astype(F32), jnp.zeros((32, C2), F32)], axis=0)
    t2 = jnp.concatenate([t2, jnp.zeros((896, C2), F32)], axis=1).T[0:C2]
    t2 = jnp.concatenate([t2, jnp.zeros((C2, 640), F32)], axis=1)
    for xo in range(3):
        w2big[xo * C2 : (xo + 1) * C2, :] = (pltpu.roll(t2, 288 * xo, 1) if xo else t2).astype(BF)
    w3t[:, 0:1728] = w3[...].reshape(1728, C3).astype(F32).T.astype(BF)
    w3t[:, 1728:1792] = jnp.zeros((C3, 64), BF)
    for kx in range(3):
        for t in range(9):
            ky, kz = 2 - t // 3, 2 - t % 3
            w3b[kx * C2 : (kx + 1) * C2, t * C3 : (t + 1) * C3] = w3[kx, ky, kz]
        for t in range(0, 10, 2):
            left = w2[kx, 2 - t // 3, 2 - t % 3].astype(F32)
            right = w2[kx, 2 - (t + 1) // 3, 2 - (t + 1) % 3].astype(F32) if t < 8 else jnp.zeros((C1, C2), F32)
            w2b[kx * C1 : (kx + 1) * C1, t * C2 : (t + 2) * C2] = jnp.concatenate([left, right], axis=1).astype(BF)

    for j, ok, dev, away in sources:
        @pl.when(ok)
        def _():
            pltpu.make_async_copy(vols.at[3 + j], vols.at[3 + j], vr.at[3 + j]).wait()

        @pl.when(jnp.logical_not(ok))
        def _():
            vols[3 + j] = jnp.zeros((C0, YS, ZS), BF)
    volf[0:224, :] = vols[...].astype(F32).reshape(224, ZS)
    for yy in range(YS):
        spread(s1, 0, volf[pl.ds(yy, 32, stride=YS), :], yy, lane)

    pre[0:160, :] = jnp.dot(w1big[...], s1[...], preferred_element_type=F32)
    for xo in range(5):
        plane = q + xo - 2
        live = jnp.where((plane >= 0) & (plane < NX), 1.0, 0.0).astype(F32)
        for yy in range(YS):
            u = pre[xo * C1 : (xo + 1) * C1, yy * ZS : (yy + 1) * ZS] + bcols[0:C1, :]
            a, e = leaky(u)
            if xo == 2:
                sl1[:, yy * ZS : (yy + 1) * ZS] = slope_from(u, e)
            spread(q1, xo * 288, a if xo == 2 else a * live, yy, lane)

    pre[0:192, :] = jnp.dot(w2big[...], q1[...], preferred_element_type=F32)
    for xo in range(3):
        plane = q + xo - 1
        live = jnp.where((plane >= 0) & (plane < NX), 1.0, 0.0).astype(F32)
        for yy in range(YS):
            u = pre[xo * C2 : (xo + 1) * C2, yy * ZS : (yy + 1) * ZS] + bcols[C2 : 2 * C2, :]
            a, e = leaky(u)
            if xo == 1:
                sl2[:, yy * ZS : (yy + 1) * ZS] = slope_from(u, e)
            spread(q2, xo * 576, a if xo == 1 else a * live, yy, lane)

    pre[0:C3, :] = jnp.dot(w3t[...], q2[...], preferred_element_type=F32)
    pltpu.make_async_copy(cotv, cotv, cr).wait()
    cotf[...] = cotv[...].astype(F32).reshape(C3 * YS, ZS)
    for yy in range(YS):
        u = pre[0:C3, yy * ZS : (yy + 1) * ZS] + b3col
        e = jnp.exp(-jnp.abs(u))
        delta = cotf[pl.ds(yy, C3, stride=YS), :] * SCALE * slope_from(u, e)
        d3[:, yy * ZS : (yy + 1) * ZS] = delta.astype(BF)
        spread(r3, 0, delta, yy, lane)

    up = q + 1 < NX
    down = q >= 1
    up_s, up_p = home(zh, y, work_c, q + 1)
    dn_s, dn_p = home(zh, y, work_c, q - 1 + 4 * (1 - jnp.minimum(q, 1)))

    def halo(tx, rx, sem):
        lower = pltpu.make_async_remote_copy(
            src_ref=tx.at[0], dst_ref=rx.at[0], send_sem=fs.at[sem], recv_sem=fr.at[sem],
            device_id=(dn_s, dn_p), device_id_type=MESH)
        upper = pltpu.make_async_remote_copy(
            src_ref=tx.at[1], dst_ref=rx.at[1], send_sem=fs.at[sem + 1], recv_sem=fr.at[sem + 1],
            device_id=(up_s, up_p), device_id_type=MESH)
        return lower, upper

    def halo_start(pair):
        pl.when(down)(pair[0].start)
        pl.when(up)(pair[1].start)

    def halo_wait(pair, rx):
        pl.when(up)(pair[0].wait_recv)
        pl.when(down)(pair[1].wait_recv)

        @pl.when(jnp.logical_not(up))
        def _():
            rx[0] = jnp.zeros(rx.shape[1:], BF)

        @pl.when(jnp.logical_not(down))
        def _():
            rx[1] = jnp.zeros(rx.shape[1:], BF)

    fl[...] = jnp.dot(w3b[...], r3[...], preferred_element_type=F32)
    tx2[0] = fl[0:C2, :].astype(BF)
    tx2[1] = fl[2 * C2 : 3 * C2, :].astype(BF)
    pair2 = halo(tx2, rx2, 0)
    halo_start(pair2)

    acc_a[0:1744, :] = lax.dot_general(q2[0:1744, :], d3[...], NT, preferred_element_type=F32).astype(BF)
    other = pl.multiple_of((1 - c) * 1024, 1024)
    mine = pl.multiple_of(c * 1024, 1024)
    copy_a0 = pltpu.make_async_remote_copy(
        src_ref=acc_a.at[pl.ds(other, 1024)], dst_ref=rx_a0, send_sem=a_s.at[0], recv_sem=a_r.at[0],
        device_id=partner, device_id_type=MESH)
    copy_a0.start()

    def xy_scatter(total, rx, send_sem, recv_sem):
        for d in range(1, 16):
            r, dev = xy_peer(d)
            pltpu.make_async_remote_copy(
                src_ref=total.at[r], dst_ref=rx.at[d - 1], send_sem=send_sem, recv_sem=recv_sem,
                device_id=dev, device_id_type=MESH).start()

    def xy_gather(buf, send_sem, recv_sem):
        for d in range(1, 16):
            _, dev = xy_peer(d)
            pltpu.make_async_remote_copy(
                src_ref=buf.at[rank], dst_ref=buf.at[rank], send_sem=send_sem, recv_sem=recv_sem,
                device_id=dev, device_id_type=MESH).start()

    def z_gather(buf, send_sem, recv_sem):
        for d in range(1, 8):
            pltpu.make_async_remote_copy(
                src_ref=buf.at[zi], dst_ref=buf.at[zi], send_sem=send_sem, recv_sem=recv_sem,
                device_id=z_peer(d), device_id_type=MESH).start()

    def wait_bytes(ref, sem):
        pltpu.make_async_copy(ref, ref, sem).wait()

    def total_of(ref, n):
        t = ref[0].astype(F32)
        for i in range(1, n):
            t = t + ref[i].astype(F32)
        return t

    copy_a0.wait_recv()
    sum_a[...] = (acc_a[pl.ds(mine, 1024), :].astype(F32) + rx_a0[...].astype(F32)).astype(BF).reshape(16, 64, ZS)
    xy_scatter(sum_a, rx_a1, a_s.at[1], a_r.at[1])

    halo_wait(pair2, rx2)
    for yy in range(YS):
        cut = slice(yy * ZS, (yy + 1) * ZS)
        flow = fl[C2 : 2 * C2, cut] + rx2[0, :, cut].astype(F32) + rx2[1, :, cut].astype(F32)
        delta = flow * sl2[:, cut]
        d2[:, cut] = delta.astype(BF)
        spread(r2, 0, delta, yy, lane)
    fl[0 : 3 * C1, :] = jnp.dot(w2b[...], r2[...], preferred_element_type=F32)
    tx1[0] = fl[0:C1, :].astype(BF)
    tx1[1] = fl[2 * C1 : 3 * C1, :].astype(BF)
    pair1 = halo(tx1, rx1, 2)
    halo_start(pair1)

    g2[0:864, :] = lax.dot_general(q1[288:1152, :], d2[...], NT, preferred_element_type=F32)
    g2[864:896, :] = lax.dot_general(s1[288:320, :], d2[...], NT, preferred_element_type=F32)
    for i in range(14):
        both = jnp.concatenate([g2[64 * i : 64 * i + 32, :], g2[64 * i + 32 : 64 * i + 64, :]], axis=1)
        acc_b[i] = both.astype(BF)
    acc_b[14] = jnp.zeros((32, ZS), BF)
    acc_b[15] = jnp.zeros((32, ZS), BF)
    copy_b0 = pltpu.make_async_remote_copy(
        src_ref=acc_b, dst_ref=rx_b0, send_sem=b_s.at[0], recv_sem=b_r.at[0], device_id=partner, device_id_type=MESH)
    copy_b0.start()
    copy_b0.wait_recv()
    sum_b[...] = (acc_b[...].astype(F32) + rx_b0[...].astype(F32)).astype(BF)
    xy_scatter(sum_b, rx_b1, b_s.at[1], b_r.at[1])

    halo_wait(pair1, rx1)
    for yy in range(YS):
        cut = slice(yy * ZS, (yy + 1) * ZS)
        flow = fl[C1 : 2 * C1, cut] + rx1[0, :, cut].astype(F32) + rx1[1, :, cut].astype(F32)
        d1[:, cut] = (flow * sl1[:, cut]).astype(BF)
    g1[...] = lax.dot_general(s1[0:320, :], d1[...], NT, preferred_element_type=F32)
    for g in range(3):
        parts = []
        for i in range(4):
            b = 4 * g + i
            if b < 9:
                parts.append(g1[b * 32 + 8 : b * 32 + 24, :])
            elif b == 9:
                parts.append(g1[288:304, :])
            else:
                parts.append(jnp.zeros((16, C1), F32))
        acc_c[g * 16 : (g + 1) * 16, :] = jnp.concatenate(parts, axis=1).astype(BF)
    copy_c0 = pltpu.make_async_remote_copy(
        src_ref=acc_c, dst_ref=rx_c0, send_sem=c_s.at[0], recv_sem=c_r.at[0], device_id=partner, device_id_type=MESH)
    copy_c0.start()
    copy_c0.wait_recv()
    x_c[rank] = (acc_c[...].astype(F32) + rx_c0[...].astype(F32)).astype(BF)
    xy_gather(x_c, c_s.at[1], c_r.at[1])

    wait_bytes(rx_a1, a_r.at[1])
    z_a[zi] = (sum_a[rank].astype(F32) + total_of(rx_a1, 15)).astype(BF)
    z_gather(z_a, a_s.at[2], a_r.at[2])
    wait_bytes(rx_b1, b_r.at[1])
    z_b[zi] = (sum_b[rank].astype(F32) + total_of(rx_b1, 15)).astype(BF)
    z_gather(z_b, b_s.at[2], b_r.at[2])
    wait_bytes(x_c.at[pl.ds(0, 15)], c_r.at[1])
    z_c[zi] = total_of(x_c, 16).astype(BF)
    z_gather(z_c, c_s.at[2], c_r.at[2])
    wait_bytes(z_a.at[pl.ds(0, 7)], a_r.at[2])
    half = gath_a.at[c]
    half[rank] = total_of(z_a, 8).astype(BF)
    xy_gather(half, a_s.at[3], a_r.at[3])
    wait_bytes(z_b.at[pl.ds(0, 7)], b_r.at[2])
    gath_b[rank] = total_of(z_b, 8).astype(BF)
    xy_gather(gath_b, b_s.at[3], b_r.at[3])

    wait_bytes(z_c.at[pl.ds(0, 7)], c_r.at[2])
    fin = total_of(z_c, 8)
    for b in range(9):
        g, i = b // 4, b % 4
        for kx in range(3):
            o1[kx, b // 3, b % 3] = fin[g * 16 + kx * 4 : g * 16 + kx * 4 + 4, i * 32 : i * 32 + 32]
    ob1[...] = fin[32:33, 32:64].reshape(C1)

    wait_bytes(half.at[pl.ds(0, 15)], a_r.at[3])
    copy_a4 = pltpu.make_async_remote_copy(
        src_ref=half, dst_ref=half, send_sem=a_s.at[4], recv_sem=a_r.at[4], device_id=partner, device_id_type=MESH)
    copy_a4.start()

    wait_bytes(gath_b.at[pl.ds(0, 15)], b_r.at[3])
    for t in range(27):
        i, s = t // 2, (t % 2) * 64
        o2[t // 9, (t // 3) % 3, t % 3] = gath_b[i].astype(F32)[:, s : s + 64]
    ob2[...] = gath_b[13].astype(F32)[0:1, 64:128].reshape(C2)

    copy_a4.wait_recv()
    for t in range(27):
        o3[t // 9, (t // 3) % 3, t % 3] = gath_a[t // 16, t % 16].astype(F32)
    ob3[...] = gath_a[1, 11].astype(F32)[0:1, :].reshape(C3)

    for j, remote, local, dev in targets:
        pl.when(remote)(vol_copy(j, dev).wait_send)
    pl.when(cot_remote)(cot_out.wait_send)
    for pair in (pair2, pair1):
        pl.when(down)(pair[0].wait_send)
        pl.when(up)(pair[1].wait_send)
    copy_a0.wait_send()
    copy_a4.wait_send()
    copy_b0.wait_send()
    copy_c0.wait_send()
    wait_bytes(rx_a1, a_s.at[1])
    wait_bytes(z_a.at[pl.ds(0, 7)], a_s.at[2])
    wait_bytes(half.at[pl.ds(0, 15)], a_s.at[3])
    wait_bytes(rx_b1, b_s.at[1])
    wait_bytes(z_b.at[pl.ds(0, 7)], b_s.at[2])
    wait_bytes(gath_b.at[pl.ds(0, 15)], b_s.at[3])
    wait_bytes(x_c.at[pl.ds(0, 15)], c_s.at[1])
    wait_bytes(z_c.at[pl.ds(0, 7)], c_s.at[2])


def local(*args):
    V = pltpu.VMEM
    D = pltpu.SemaphoreType.DMA
    vm = pl.BlockSpec(memory_space=pltpu.VMEM)
    shapes = (
        ((3, 3, 3, C0, C1), F32), ((C1,), F32), ((3, 3, 3, C1, C2), F32), ((C2,), F32), ((3, 3, 3, C2, C3), F32), ((C3,), F32),
    )
    return pl.pallas_call(
        body,
        out_shape=tuple(jax.ShapeDtypeStruct(s, d) for s, d in shapes),
        in_specs=[vm, pl.BlockSpec(memory_space=pl.ANY), vm, vm, vm, vm, vm, vm],
        out_specs=(vm,) * 6,
        scratch_shapes=[
            V((7, C0, YS, ZS), BF), V((C3, YS, ZS), BF), V((C3 * YS, ZS), F32), V((256, ZS), F32),
            V((384, ZS), F32), V((160, 384), BF), V((192, 1536), BF), V((C3, 1792), BF), V((192, 1152), BF), V((96, 640), BF),
            V((ZS, ZS), F32),
            V((384, CELLS), BF), V((1536, CELLS), BF), V((1792, CELLS), BF), V((1152, CELLS), BF), V((640, CELLS), BF),
            V((192, CELLS), F32), V((C3, CELLS), BF), V((C2, CELLS), BF), V((C1, CELLS), BF), V((C1, CELLS), F32), V((C2, CELLS), F32),
            V((192, CELLS), F32), V((2, C2, CELLS), BF), V((2, C2, CELLS), BF), V((2, C1, CELLS), BF), V((2, C1, CELLS), BF),
            V((2048, ZS), BF), V((1024, ZS), BF), V((16, 64, ZS), BF), V((15, 64, ZS), BF), V((8, 64, ZS), BF), V((2, 16, 64, ZS), BF),
            V((896, C2), F32), V((16, 32, ZS), BF), V((16, 32, ZS), BF), V((16, 32, ZS), BF), V((15, 32, ZS), BF), V((8, 32, ZS), BF),
            V((16, 32, ZS), BF),
            V((320, C1), F32), V((48, ZS), BF), V((48, ZS), BF), V((16, 48, ZS), BF), V((8, 48, ZS), BF),
            D((7,)), D((7,)), D, D, D((4,)), D((4,)), D((5,)), D((5,)), D((4,)), D((4,)), D((3,)), D((3,)),
        ],
        compiler_params=pltpu.CompilerParams(collective_id=0, has_side_effects=True, vmem_limit_bytes=48 << 20),
        name="backward",
    )(*args)


def solution(mesh):
    placed = (
        P("sample", None, "space", None, None),
        P("sample", None, "space", None, None),
        P(), P(), P(), P(), P(), P(),
    )
    return jax.shard_map(local, mesh=mesh, in_specs=placed, out_specs=(P(),) * 6, check_vma=False)
```

time: 369 us -> 56.5 us (0.15)
  waiting for transfers between devices: 175 us -> 0 us
  blocking collectives: 92.9 us -> 0 us
  Pallas kernels: 0 us -> 45.4 us
  matrix products: 34.7 us -> 0 us
  starting transfers between devices: 33.4 us -> 0 us
  between operations: 15.5 us -> 0.66 us
  other arithmetic: 3.83 us -> 0 us
    psum x1 -> x0, waiting for transfers between devices: 173 us -> none  [local(): lax.psum((grads[0], grads[1], grads[2], grads[3], grads[4], grads[5]), ('...]
    psum x1 -> x0, blocking collectives: 92.9 us -> none  [local(): lax.psum((grads[0], grads[1], grads[2], grads[3], grads[4], grads[5]), ('...]
    pallas_call x0 -> x1, Pallas kernels: none -> 45.4 us  [local(): pl.pallas_call(body, out_shape=tuple((jax.ShapeDtypeStruct(s, d) for s, d...]
    dot_general x164 -> x0, matrix products: 34.7 us -> none  [the longest x54 14.1 us: conv_taps(): lax.dot_general(weight[along_x, along_y, along_z], window, (((0,), (0,)),...]
    ppermute x10 -> x0, starting transfers between devices: 33.4 us -> none  [the longest x5 26.9 us: with_halo(): before = lax.ppermute(last, axis, up)]
    slice x8 -> x0, local copies, waits for them, and re-layouts: 3.82 us -> none  [the longest x4 2.25 us: transpose_taps(): padded[:, start_x:start_x + size_x, start_y:start_y + size_y, start_z:sta...]
    concatenate x5 -> x0, other arithmetic: 3.79 us -> none  [with_halo(): array = jnp.concatenate([before, array, after], axis=dim)]
    unnamed x70 -> x22, local copies, waits for them, and re-layouts: 7.13 us -> 10.1 us
  transfers between devices with their start and end apart: 11 -> 0, of which waited for: 3 -> 0; matrix products, arithmetic and copies ran while one was open for 5% -> 0% of each run, Pallas kernels for 0% -> 0%
where the time goes in v1:
time: 56.5 us; the launch traced here: 56.2 us
  Pallas kernels  45.4 us (80%)
  local copies, waits for them, and re-layouts  10.1 us (18%)
  between operations  0.66 us (1%)
    pallas_call x1, Pallas kernels, local(): pl.pallas_call(body, out_shape=tuple((jax.ShapeDtypeStruct(s, d) for s, d...  45.4 us
    unnamed x22, local copies, waits for them, and re-layouts  10.1 us

profile of v1, /device:TPU:1, one launch (start us, length us, event | category | flops | bytes accessed | tf_op | source)
XLA Modules:
  0.0 56.2 jit_solution(1319110808953710619)
XLA Ops:
  0.6 0.0 copy-start
  0.6 1.0 %copy-done = bf16[3,3,3,64,128]{4,3,2,1,0:T(8,128)(2,1)S(1)} copy-done((bf16[3,3,3,64,128]{4,3,2,1,0:T(8,128)(2,1)S(1)}, bf16[3,3,3,64,128]{4,3,2,1,0:T(8,128)(2,1)}, u32[]{:S(2)}) %copy-start) | copy-done | bytes 442392
  1.6 0.0 copy-start.1
  1.7 0.9 %copy-done.1 = bf16[1,128,1,8,128]{4,3,2,1,0:T(8,128)(2,1)S(1)} copy-done((bf16[1,128,1,8,128]{4,3,2,1,0:T(8,128)(2,1)S(1)}, bf16[1,128,1,8,128]{4,3,2,1,0:T(8,128)(2,1)}, u32[]{:S(2)}) %copy-start.1) | copy-done | bytes 262168
  2.6 0.0 copy-start.2
  2.6 0.9 %copy-done.2 = bf16[3,3,3,32,64]{4,3,2,1,0:T(8,128)(2,1)S(1)} copy-done((bf16[3,3,3,32,64]{4,3,2,1,0:T(8,128)(2,1)S(1)}, bf16[3,3,3,32,64]{4,3,2,1,0:T(8,128)(2,1)}, u32[]{:S(2)}) %copy-start.2) | copy-done | bytes 110616
  3.5 0.0 copy-start.3
  3.5 0.7 %copy-done.3 = bf16[3,3,3,4,32]{4,3,2,1,0:T(4,128)(2,1)S(1)} copy-done((bf16[3,3,3,4,32]{4,3,2,1,0:T(4,128)(2,1)S(1)}, bf16[3,3,3,4,32]{4,3,2,1,0:T(4,128)(2,1)}, u32[]{:S(2)}) %copy-start.3) | copy-done | bytes 6936
  4.3 0.0 copy-start.4
  4.3 0.7 %copy-done.4 = bf16[1,4,1,8,128]{4,3,2,1,0:T(8,128)(2,1)S(1)} copy-done((bf16[1,4,1,8,128]{4,3,2,1,0:T(8,128)(2,1)S(1)}, bf16[1,4,1,8,128]{4,3,2,1,0:T(8,128)(2,1)}, u32[]{:S(2)}) %copy-start.4) | copy-done | bytes 8216
  5.0 0.0 copy-start.5
  5.0 0.7 %copy-done.5 = f32[32]{0:T(128)S(1)} copy-done((f32[32]{0:T(128)S(1)}, f32[32]{0:T(128)}, u32[]{:S(2)}) %copy-start.5) | copy-done | bytes 152
  5.6 0.0 copy-start.6
  5.6 0.7 %copy-done.6 = f32[64]{0:T(128)S(1)} copy-done((f32[64]{0:T(128)S(1)}, f32[64]{0:T(128)}, u32[]{:S(2)}) %copy-start.6) | copy-done | bytes 280
  6.3 0.0 copy-start.7
  6.3 0.7 %copy-done.7 = f32[128]{0:T(128)S(1)} copy-done((f32[128]{0:T(128)S(1)}, f32[128]{0:T(128)}, u32[]{:S(2)}) %copy-start.7) | copy-done | bytes 536
  6.9 45.4 %backward.1 = (f32[3,3,3,4,32]{4,3,2,1,0:T(4,128)S(1)}, f32[32]{0:T(128)S(1)}, f32[3,3,3,32,64]{4,3,2,1,0:T(8,128)S(1)}, f32[64]{0:T(128)S(1)}, f32[3,3,3,64,128]{4,3,2,1,0:T(8,128)S(1)}, /*index=5*/f32[128]{0:T(128)S(1)}) custom-call(bf16[1,4,1,8,128]{4,3,2,1,0:T(8,128)(2,1)S(1)} %copy-done.4, bf16[1,128,1,8,128]{4,3,2,1,0:T(8,128)(2,1)S(1)} %copy-done.1, ...), custom_call_target="tpu_custom_call" | custom-call | tf_op jit(solution)/shard_map/backward/pallas_call | solution.py:426
  52.4 0.6 %copy.20 = f32[3,3,3,4,32]{4,3,2,1,0:T(4,128)} copy(f32[3,3,3,4,32]{4,3,2,1,0:T(4,128)S(1)} %get-tuple-element.12) | data formatting | bytes 27648
  53.0 0.5 copy.21
  53.5 0.8 %copy.22 = f32[3,3,3,32,64]{4,3,2,1,0:T(8,128)} copy(f32[3,3,3,32,64]{4,3,2,1,0:T(8,128)S(1)} %get-tuple-element.14) | data formatting | bytes 442368
  54.3 0.5 copy.23
  54.8 0.9 %copy.24 = f32[3,3,3,64,128]{4,3,2,1,0:T(8,128)} copy(f32[3,3,3,64,128]{4,3,2,1,0:T(8,128)S(1)} %get-tuple-element.16) | data formatting | bytes 1769472
  55.7 0.5 copy.25
Async XLA Ops:
  0.6 1.0 %copy-start = (bf16[3,3,3,64,128]{4,3,2,1,0:T(8,128)(2,1)S(1)}, bf16[3,3,3,64,128]{4,3,2,1,0:T(8,128)(2,1)}, u32[]{:S(2)}) copy-start(bf16[3,3,3,64,128]{4,3,2,1,0:T(8,128)(2,1)} %w3.1) | copy-start | bytes 1327108
  1.6 0.9 %copy-start.1 = (bf16[1,128,1,8,128]{4,3,2,1,0:T(8,128)(2,1)S(1)}, bf16[1,128,1,8,128]{4,3,2,1,0:T(8,128)(2,1)}, u32[]{:S(2)}) copy-start(bf16[1,128,1,8,128]{4,3,2,1,0:T(8,128)(2,1)} %cot.1) | copy-start | bytes 786436
  2.6 0.9 %copy-start.2 = (bf16[3,3,3,32,64]{4,3,2,1,0:T(8,128)(2,1)S(1)}, bf16[3,3,3,32,64]{4,3,2,1,0:T(8,128)(2,1)}, u32[]{:S(2)}) copy-start(bf16[3,3,3,32,64]{4,3,2,1,0:T(8,128)(2,1)} %w2.1) | copy-start | bytes 331780
  3.5 0.7 %copy-start.3 = (bf16[3,3,3,4,32]{4,3,2,1,0:T(4,128)(2,1)S(1)}, bf16[3,3,3,4,32]{4,3,2,1,0:T(4,128)(2,1)}, u32[]{:S(2)}) copy-start(bf16[3,3,3,4,32]{4,3,2,1,0:T(4,128)(2,1)} %w1.1) | copy-start | bytes 20740
  4.3 0.7 %copy-start.4 = (bf16[1,4,1,8,128]{4,3,2,1,0:T(8,128)(2,1)S(1)}, bf16[1,4,1,8,128]{4,3,2,1,0:T(8,128)(2,1)}, u32[]{:S(2)}) copy-start(bf16[1,4,1,8,128]{4,3,2,1,0:T(8,128)(2,1)} %vol.1) | copy-start | bytes 24580
  5.0 0.7 %copy-start.5 = (f32[32]{0:T(128)S(1)}, f32[32]{0:T(128)}, u32[]{:S(2)}) copy-start(f32[32]{0:T(128)} %b1.1) | copy-start | bytes 388
  5.6 0.7 %copy-start.6 = (f32[64]{0:T(128)S(1)}, f32[64]{0:T(128)}, u32[]{:S(2)}) copy-start(f32[64]{0:T(128)} %b2.1) | copy-start | bytes 772
  6.3 0.7 %copy-start.7 = (f32[128]{0:T(128)S(1)}, f32[128]{0:T(128)}, u32[]{:S(2)}) copy-start(f32[128]{0:T(128)} %b3.1) | copy-start | bytes 1540

commit v2 on v1

v2 whole, which is shorter than its diff:
```python
import math

import jax
import jax.numpy as jnp
from jax import lax
from jax.experimental import pallas as pl
from jax.experimental.pallas import tpu as pltpu
from jax.sharding import PartitionSpec as P

MESH = pl.DeviceIdType.MESH
BF = jnp.bfloat16
F32 = jnp.float32

C0, C1, C2, C3 = 4, 32, 64, 128
YS, ZS, NX = 8, 128, 16
CELLS = YS * ZS
SCALE = 1.0 / math.sqrt(16 * NX * YS * ZS)
NT = (((1,), (1,)), ((), ()))


def softplus_sigmoid(u):
    e = jnp.exp(-jnp.abs(u))
    return jnp.maximum(u, 0.0) + jnp.log(1.0 + e), e


def leaky(u):
    soft, e = softplus_sigmoid(u)
    return 0.3 * u + 0.7 * soft, e


def slope_from(u, e):
    r = 1.0 / (1.0 + e)
    return 0.3 + 0.7 * jnp.where(u >= 0.0, r, e * r)


def shifted(slab, lane):
    lo = jnp.where(lane == 0, 0.0, pltpu.roll(slab, 1, 1))
    hi = jnp.where(lane == ZS - 1, 0.0, pltpu.roll(slab, ZS - 1, 1))
    return lo.astype(BF), slab.astype(BF), hi.astype(BF)


def spread(ref, base, slab, ysrc, lane):
    width = slab.shape[0]
    parts = shifted(slab, lane)
    for ky in range(3):
        yo = ysrc + 1 - ky
        if 0 <= yo < YS:
            for kz in range(3):
                row = base + (ky * 3 + kz) * width
                ref[row : row + width, yo * ZS : (yo + 1) * ZS] = parts[kz]


def zero_edges(ref, base, width):
    for ky, yo in ((0, 0), (2, YS - 1)):
        row = base + ky * 3 * width
        ref[row : row + 3 * width, yo * ZS : (yo + 1) * ZS] = jnp.zeros((3 * width, ZS), BF)


def body(
    vol_h, cot, w1_h, b1_h, w2_h, b2_h, w3_h, b3_h,
    out_a, out_b,
    gath_a, gath_b, outs,
    vol, w1, b1, w2, b2, w3, b3, ins,
    vols, cotv, cotf, volf, w1f, w1big, w2big, w3t, w3b, w2b, bcols,
    s1, q1, q2, r3, r2, pre, d3, d2, d1, sl1, sl2, fl,
    acc_a, own_a, rx_a0, sum_a, rx_a1, z_a,
    g2, acc_b, rx_b0, sum_b, rx_b1, z_b,
    g1,
    vs, vr, a_s, a_r, b_s, b_r, ready,
):
    me_s, me_p = lax.axis_index("sample"), lax.axis_index("space")
    zh, y, c = me_s // 8, (me_s // 2) % 4, me_s % 2
    x, zl = me_p // 4, me_p % 4
    rank = x * 4 + y
    zi = zh * 4 + zl
    partner = (me_s + 1 - 2 * c, me_p)

    def xy_peer(d):
        r = (rank + d) % 16
        return r, (zh * 8 + (r % 4) * 2 + c, (r // 4) * 4 + zl)

    def z_peer(d):
        z = (zi + d) % 8
        return ((z // 4) * 8 + y * 2 + c, x * 4 + z % 4)

    near = [(j, (me_p + j >= 0) & (me_p + j < NX)) for j in (1, -1, 2, -2, 3, -3)]

    leaving = []

    x_line = [(me_s, (me_p + 4 * d) % 16) for d in (2, 1, 3)]
    y_line = [(zh * 8 + ((y + d) % 4) * 2 + c, me_p) for d in (2, 1, 3)]
    z_line = [(me_s, 4 * x + (zl + d) % 4) for d in (1, 2, 3)]
    barrier = pltpu.get_barrier_semaphore()
    count = jnp.int32(8)
    for j, ok in near[::-1]:
        @pl.when(ok)
        def _():
            pl.semaphore_signal(barrier, 1, device_id=(me_s, me_p + j), device_id_type=MESH)
        count = count + ok.astype(jnp.int32)
    for dev in [((me_s + 8) % 16, me_p)] + x_line + y_line + [partner]:
        pl.semaphore_signal(barrier, 1, device_id=dev, device_id_type=MESH)

    loads = [
        pltpu.make_async_copy(src, dst, ins.at[i])
        for i, (src, dst) in enumerate(((w1_h, w1), (b1_h, b1), (b2_h, b2), (b3_h, b3), (vol_h, vol), (w2_h, w2), (w3_h, w3), (cot, cotv)))
    ]
    for load in loads:
        load.start()

    lane = lax.broadcasted_iota(jnp.int32, (1, ZS), 1)
    loads[4].wait()
    pl.semaphore_wait(barrier, count)


    for j, ok in near:
        copy = pltpu.make_async_remote_copy(
            src_ref=vol.at[0, :, 0], dst_ref=vols.at[3 - j], send_sem=vs.at[3 + j], recv_sem=vr.at[3 - j],
            device_id=(me_s, me_p + j), device_id_type=MESH)
        pl.when(ok)(copy.start)
        leaving.append((ok, copy.wait_send))

    for dev in x_line + z_line:
        pl.semaphore_signal(ready, 1, device_id=dev, device_id_type=MESH)

    w1f[...] = jnp.zeros_like(w1f)
    for load in loads[:4]:
        load.wait()
    for kx in range(3):
        for ky in range(3):
            for kz in range(3):
                row = (ky * 3 + kz) * 32 + kx * 4
                w1f[row : row + 4, 0:C1] = w1[kx, ky, kz].astype(F32)
    t1 = w1f[...].T[0:C1]
    for xo in range(5):
        w1big[xo * C1 : (xo + 1) * C1, :] = (pltpu.roll(t1, 4 * xo, 1) if xo else t1).astype(BF)
    bcols[...] = jnp.zeros_like(bcols)
    bcols[:, 0:C1] = jnp.broadcast_to(b1[...].reshape(1, C1), (ZS, C1))
    bcols[:, C2 : 2 * C2] = jnp.broadcast_to(b2[...].reshape(1, C2), (ZS, C2))
    bt = bcols[...].T
    bcols[...] = bt
    b3col = jnp.broadcast_to(b3[...].reshape(1, C3), (ZS, C3)).T
    s1[288:320, :] = jnp.ones((32, CELLS), BF)
    s1[320:384, :] = jnp.zeros((64, CELLS), BF)
    zero_edges(s1, 0, 32)
    for xo in range(5):
        zero_edges(q1, xo * 288, C1)
    q1[1440:1536, :] = jnp.zeros((96, CELLS), BF)
    for xo in range(3):
        zero_edges(q2, xo * 576, C2)
    q2[1728:1744, :] = jnp.ones((16, CELLS), BF)
    q2[1744:2048, :] = jnp.zeros((304, CELLS), BF)
    zero_edges(r3, 0, C3)
    for xo in range(3):
        zero_edges(r2, xo * 576, C2)
    r2[1728:1792, :] = jnp.zeros((64, CELLS), BF)
    volf[224:256, :] = jnp.zeros((32, ZS), F32)

    for load in loads[5:]:
        load.wait()
    vols[3] = vol[0, :, 0]
    cotf[...] = cotv[...].reshape(C3, YS, ZS).astype(F32).reshape(C3 * YS, ZS)
    t2 = jnp.concatenate([w2[...].reshape(864, C2).astype(F32), jnp.zeros((32, C2), F32)], axis=0)
    t2 = jnp.concatenate([t2, jnp.zeros((896, C2), F32)], axis=1).T[0:C2]
    t2 = jnp.concatenate([t2, jnp.zeros((C2, 640), F32)], axis=1)
    for xo in range(3):
        w2big[xo * C2 : (xo + 1) * C2, :] = (pltpu.roll(t2, 288 * xo, 1) if xo else t2).astype(BF)
    w3t[:, 0:1728] = w3[...].reshape(1728, C3).astype(F32).T.astype(BF)
    w3t[:, 1728:1792] = jnp.zeros((C3, 64), BF)
    for kx in range(3):
        for t in range(9):
            ky, kz = 2 - t // 3, 2 - t % 3
            w3b[kx * C2 : (kx + 1) * C2, t * C3 : (t + 1) * C3] = w3[kx, ky, kz]
    def back_tap(xo, n):
        plane, t = n // 9, n % 9
        kx = xo - plane
        if n >= 27 or not 0 <= kx < 3:
            return jnp.zeros((C1, C2), F32)
        return w2[kx, 2 - t // 3, 2 - t % 3].astype(F32)

    for xo in range(5):
        for n in range(0, 28, 2):
            both = jnp.concatenate([back_tap(xo, n), back_tap(xo, n + 1)], axis=1)
            w2b[xo * C1 : (xo + 1) * C1, n * C2 : (n + 2) * C2] = both.astype(BF)

    pl.semaphore_wait(ready, 6)

    for j, ok in near:
        @pl.when(ok)
        def _():
            pltpu.make_async_copy(vols.at[3 + j], vols.at[3 + j], vr.at[3 + j]).wait()

        @pl.when(jnp.logical_not(ok))
        def _():
            vols[3 + j] = jnp.zeros((C0, YS, ZS), BF)
    volf[0:224, :] = vols[...].astype(F32).reshape(224, ZS)
    for yy in range(YS):
        spread(s1, 0, volf[pl.ds(yy, 32, stride=YS), :], yy, lane)

    pre[0:160, :] = jnp.dot(w1big[...], s1[...], preferred_element_type=F32)
    for xo in range(5):
        plane = me_p + xo - 2
        live = jnp.where((plane >= 0) & (plane < NX), 1.0, 0.0).astype(F32)
        for yy in range(YS):
            u = pre[xo * C1 : (xo + 1) * C1, yy * ZS : (yy + 1) * ZS] + bcols[0:C1, :]
            a, e = leaky(u)
            sl1[xo * C1 : (xo + 1) * C1, yy * ZS : (yy + 1) * ZS] = slope_from(u, e) * live
            spread(q1, xo * 288, a * live, yy, lane)

    pre[0:192, :] = jnp.dot(w2big[...], q1[...], preferred_element_type=F32)
    for xo in range(3):
        plane = me_p + xo - 1
        live = jnp.where((plane >= 0) & (plane < NX), 1.0, 0.0).astype(F32)
        for yy in range(YS):
            u = pre[xo * C2 : (xo + 1) * C2, yy * ZS : (yy + 1) * ZS] + bcols[C2 : 2 * C2, :]
            a, e = leaky(u)
            sl2[xo * C2 : (xo + 1) * C2, yy * ZS : (yy + 1) * ZS] = slope_from(u, e) * live
            spread(q2, xo * 576, a * live, yy, lane)

    pre[0:C3, :] = jnp.dot(w3t[...], q2[0:1792, :], preferred_element_type=F32)
    for yy in range(YS):
        u = pre[0:C3, yy * ZS : (yy + 1) * ZS] + b3col
        e = jnp.exp(-jnp.abs(u))
        delta = cotf[pl.ds(yy, C3, stride=YS), :] * SCALE * slope_from(u, e)
        d3[:, yy * ZS : (yy + 1) * ZS] = delta.astype(BF)
        spread(r3, 0, delta, yy, lane)

    def xy_scatter(total, rx, send_sem, recv_sem):
        for d in range(1, 16):
            r, dev = xy_peer(d)
            pltpu.make_async_remote_copy(
                src_ref=total.at[r], dst_ref=rx.at[d - 1], send_sem=send_sem, recv_sem=recv_sem,
                device_id=dev, device_id_type=MESH).start()
        leaving.append((True, lambda: wait_bytes(rx, send_sem)))

    def xy_gather(buf, send_sem, recv_sem):
        for d in range(1, 16):
            _, dev = xy_peer(d)
            pltpu.make_async_remote_copy(
                src_ref=buf.at[rank], dst_ref=buf.at[rank], send_sem=send_sem, recv_sem=recv_sem,
                device_id=dev, device_id_type=MESH).start()
        leaving.append((True, lambda: wait_bytes(buf.at[pl.ds(0, 15)], send_sem)))

    def z_gather(buf, send_sem, recv_sem):
        for d in range(1, 8):
            pltpu.make_async_remote_copy(
                src_ref=buf.at[zi], dst_ref=buf.at[zi], send_sem=send_sem, recv_sem=recv_sem,
                device_id=z_peer(d), device_id_type=MESH).start()
        leaving.append((True, lambda: wait_bytes(buf.at[pl.ds(0, 7)], send_sem)))

    def wait_bytes(ref, sem):
        pltpu.make_async_copy(ref, ref, sem).wait()

    def total_of(ref, n):
        t = ref[0].astype(F32)
        for i in range(1, n):
            t = t + ref[i].astype(F32)
        return t

    other = pl.multiple_of((1 - c) * 1024, 1024)
    mine = pl.multiple_of(c * 1024, 1024)
    acc_a[...] = lax.dot_general(q2[pl.ds(other, 1024), :], d3[...], NT, preferred_element_type=F32).astype(BF)
    copy_a0 = pltpu.make_async_remote_copy(
        src_ref=acc_a, dst_ref=rx_a0, send_sem=a_s.at[0], recv_sem=a_r.at[0],
        device_id=partner, device_id_type=MESH)
    copy_a0.start()
    leaving.append((True, copy_a0.wait_send))

    own_a[...] = lax.dot_general(q2[pl.ds(mine, 1024), :], d3[...], NT, preferred_element_type=F32)

    fl[...] = jnp.dot(w3b[...], r3[...], preferred_element_type=F32)

    copy_a0.wait_recv()
    sum_a[...] = (own_a[...] + rx_a0[...].astype(F32)).astype(BF).reshape(16, 64, ZS)
    xy_scatter(sum_a, rx_a1, a_s.at[1], a_r.at[1])

    for xo in range(3):
        rows = slice(xo * C2, (xo + 1) * C2)
        for yy in range(YS):
            cut = slice(yy * ZS, (yy + 1) * ZS)
            delta = fl[rows, cut] * sl2[rows, cut]
            d2[rows, cut] = delta.astype(BF)
            spread(r2, xo * 576, delta, yy, lane)

    d1[...] = (jnp.dot(w2b[...], r2[...], preferred_element_type=F32) * sl1[...]).astype(BF)

    g2[0:1440, :] = lax.dot_general(q1[0:1440, :], d2[...], NT, preferred_element_type=F32)
    g2[1440:1472, :] = lax.dot_general(s1[288:320, :], d2[...], NT, preferred_element_type=F32)

    def tap_two(n):
        if n == 27:
            return sum(g2[1440:1472, p * C2 : (p + 1) * C2] for p in range(3))
        row = (n // 9) * 288 + (n % 9) * C1
        return sum(g2[row + p * 288 : row + p * 288 + C1, p * C2 : (p + 1) * C2] for p in range(3))

    def pack_b(i, rows):
        acc_b[0, i] = rows[0:16].astype(BF)
        acc_b[1, i] = rows[16:32].astype(BF)

    for i in range(14):
        pack_b(i, jnp.concatenate([tap_two(2 * i), tap_two(2 * i + 1)], axis=1))

    g1[...] = lax.dot_general(s1[0:320, :], d1[...], NT, preferred_element_type=F32)

    def tap_one(b):
        if b > 9:
            return jnp.zeros((16, C1), F32)
        if b == 9:
            return sum(g1[288:304, p * C1 : (p + 1) * C1] for p in range(5))
        return sum(g1[b * 32 + 4 * p : b * 32 + 4 * p + 16, p * C1 : (p + 1) * C1] for p in range(5))

    rows_one = [jnp.concatenate([tap_one(4 * g + i) for i in range(4)], axis=1) for g in range(3)]
    pack_b(14, jnp.concatenate(rows_one[0:2], axis=0))
    pack_b(15, jnp.concatenate([rows_one[2], jnp.zeros((16, ZS), F32)], axis=0))
    copy_b0 = pltpu.make_async_remote_copy(
        src_ref=acc_b.at[1 - c], dst_ref=rx_b0, send_sem=b_s.at[0], recv_sem=b_r.at[0], device_id=partner, device_id_type=MESH)
    copy_b0.start()
    leaving.append((True, copy_b0.wait_send))
    copy_b0.wait_recv()
    sum_b[...] = (acc_b[c].astype(F32) + rx_b0[...].astype(F32)).astype(BF)
    xy_scatter(sum_b, rx_b1, b_s.at[1], b_r.at[1])

    wait_bytes(rx_a1, a_r.at[1])
    z_a[zi] = (sum_a[rank].astype(F32) + total_of(rx_a1, 15)).astype(BF)
    z_gather(z_a, a_s.at[2], a_r.at[2])
    wait_bytes(rx_b1, b_r.at[1])
    z_b[zi] = (sum_b[rank].astype(F32) + total_of(rx_b1, 15)).astype(BF)
    z_gather(z_b, b_s.at[2], b_r.at[2])
    wait_bytes(z_a.at[pl.ds(0, 7)], a_r.at[2])
    half = gath_a.at[c]
    half[rank] = total_of(z_a, 8).astype(BF)
    xy_gather(half, a_s.at[3], a_r.at[3])
    wait_bytes(z_b.at[pl.ds(0, 7)], b_r.at[2])
    half_b = gath_b.at[c]
    half_b[rank] = total_of(z_b, 8).astype(BF)
    xy_gather(half_b, b_s.at[3], b_r.at[3])

    def write(i, src, dst):
        copy = pltpu.make_async_copy(src, dst, outs.at[i])
        copy.start()
        leaving.append((True, copy.wait))

    wait_bytes(half.at[pl.ds(0, 15)], a_r.at[3])
    copy_a4 = pltpu.make_async_remote_copy(
        src_ref=half, dst_ref=half, send_sem=a_s.at[4], recv_sem=a_r.at[4], device_id=partner, device_id_type=MESH)
    copy_a4.start()
    leaving.append((True, copy_a4.wait_send))
    write(1, half, out_a.at[c])

    wait_bytes(half_b.at[pl.ds(0, 15)], b_r.at[3])
    copy_b4 = pltpu.make_async_remote_copy(
        src_ref=half_b, dst_ref=half_b, send_sem=b_s.at[4], recv_sem=b_r.at[4], device_id=partner, device_id_type=MESH)
    copy_b4.start()
    leaving.append((True, copy_b4.wait_send))
    copy_a4.wait_recv()
    write(2, gath_a.at[1 - c], out_a.at[1 - c])
    copy_b4.wait_recv()
    write(0, gath_b, out_b)

    for cond, wait in leaving:
        if cond is True:
            wait()
        else:
            pl.when(cond)(wait)


def unpack(in_a, in_b, o1, ob1, o2, ob2, o3, ob3, gath_a, gath_b, v1, vb1, v2, vb2, v3, vb3, sems, ins):
    pairs = ((in_a.at[0], gath_a.at[0]), (in_a.at[1], gath_a.at[1]), (in_b, gath_b))
    loads = [pltpu.make_async_copy(src, dst, ins.at[i]) for i, (src, dst) in enumerate(pairs)]
    for load in loads:
        load.start()
    outs = (o3, o2, o1, ob1, ob2, ob3)
    copies = [pltpu.make_async_copy(v, o, sems.at[i]) for i, (v, o) in enumerate(zip((v3, v2, v1, vb1, vb2, vb3), outs))]
    loads[0].wait()
    loads[1].wait()
    for t in range(27):
        v3[t // 9, (t // 3) % 3, t % 3] = gath_a[t // 16, t % 16].astype(F32)
    copies[0].start()
    loads[2].wait()

    def rows_b(i):
        return jnp.concatenate([gath_b[0, i].astype(F32), gath_b[1, i].astype(F32)], axis=0)

    for t in range(27):
        i, s = t // 2, (t % 2) * 64
        v2[t // 9, (t // 3) % 3, t % 3] = rows_b(i)[:, s : s + 64]
    copies[1].start()
    fin = jnp.concatenate([rows_b(14), rows_b(15)], axis=0)
    for b in range(9):
        g, i = b // 4, b % 4
        for kx in range(3):
            v1[kx, b // 3, b % 3] = fin[g * 16 + kx * 4 : g * 16 + kx * 4 + 4, i * 32 : i * 32 + 32]
    copies[2].start()
    vb1[...] = fin[32:33, 32:64].reshape(C1)
    copies[3].start()
    vb2[...] = rows_b(13)[0:1, 64:128].reshape(C2)
    copies[4].start()
    vb3[...] = gath_a[1, 11].astype(F32)[0:1, :].reshape(C3)
    copies[5].start()
    for copy in copies:
        copy.wait()


def local(*args):
    V = pltpu.VMEM
    D = pltpu.SemaphoreType.DMA
    hbm = pl.BlockSpec(memory_space=pltpu.HBM)
    sums = pl.pallas_call(
        body,
        out_shape=(
            jax.ShapeDtypeStruct((2, 16, 64, ZS), BF),
            jax.ShapeDtypeStruct((2, 16, 16, ZS), BF),
        ),
        in_specs=[hbm] * 8,
        out_specs=(hbm,) * 2,
        scratch_shapes=[
            V((2, 16, 64, ZS), BF), V((2, 16, 16, ZS), BF), D((3,)),
            V((1, C0, 1, YS, ZS), BF), V((3, 3, 3, C0, C1), BF), V((C1,), F32), V((3, 3, 3, C1, C2), BF), V((C2,), F32),
            V((3, 3, 3, C2, C3), BF), V((C3,), F32), D((8,)),
            V((7, C0, YS, ZS), BF), V((1, C3, 1, YS, ZS), BF), V((C3 * YS, ZS), F32), V((256, ZS), F32),
            V((384, ZS), F32), V((160, 384), BF), V((192, 1536), BF), V((C3, 1792), BF), V((192, 1152), BF), V((160, 1792), BF),
            V((ZS, ZS), F32),
            V((384, CELLS), BF), V((1536, CELLS), BF), V((2048, CELLS), BF), V((1152, CELLS), BF), V((1792, CELLS), BF),
            V((192, CELLS), F32), V((C3, CELLS), BF), V((192, CELLS), BF), V((160, CELLS), BF), V((160, CELLS), F32), V((192, CELLS), F32),
            V((192, CELLS), F32),
            V((1024, ZS), BF), V((1024, ZS), F32), V((1024, ZS), BF), V((16, 64, ZS), BF), V((15, 64, ZS), BF), V((8, 64, ZS), BF),
            V((1472, 192), F32), V((2, 16, 16, ZS), BF), V((16, 16, ZS), BF), V((16, 16, ZS), BF), V((15, 16, ZS), BF), V((8, 16, ZS), BF),
            V((320, 160), F32),
            D((7,)), D((7,)), D((5,)), D((5,)), D((5,)), D((5,)), pltpu.SemaphoreType.REGULAR,
        ],
        compiler_params=pltpu.CompilerParams(collective_id=0, has_side_effects=True, vmem_limit_bytes=62 << 20),
        name="backward",
    )(*args)
    shapes = ((3, 3, 3, C0, C1), (C1,), (3, 3, 3, C1, C2), (C2,), (3, 3, 3, C2, C3), (C3,))
    return pl.pallas_call(
        unpack,
        out_shape=tuple(jax.ShapeDtypeStruct(s, F32) for s in shapes),
        in_specs=[hbm] * 2,
        out_specs=(hbm,) * 6,
        scratch_shapes=[V((2, 16, 64, ZS), BF), V((2, 16, 16, ZS), BF)]
        + [V(s, F32) for s in shapes]
        + [D((6,)), D((3,))],
        compiler_params=pltpu.CompilerParams(vmem_limit_bytes=62 << 20),
        name="widen",
    )(*sums)


def solution(mesh):
    placed = (
        P("sample", None, "space", None, None),
        P("sample", None, "space", None, None),
        P(), P(), P(), P(), P(), P(),
    )
    return jax.shard_map(local, mesh=mesh, in_specs=placed, out_specs=(P(),) * 6, check_vma=False)
```

time: 56.5 us -> 43.1 us (0.76)
  local copies, waits for them, and re-layouts: 10.1 us -> 0 us
  Pallas kernels: 45.4 us -> 42.3 us
    unnamed x22 -> x0, local copies, waits for them, and re-layouts: 10.1 us -> none
    pallas_call x1 -> x2, Pallas kernels: 45.4 us -> 42.3 us  [the longest x1 40.1 us: local(): pl.pallas_call(body, out_shape=(jax.ShapeDtypeStruct((2, 16, 64, ZS), BF)...]
where the time goes in v2:
time: 43.1 us; the launch traced here: 43 us
  Pallas kernels  42.3 us (98%)
  between operations  0.64 us (1%)
    pallas_call x1, Pallas kernels, local(): pl.pallas_call(body, out_shape=(jax.ShapeDtypeStruct((2, 16, 64, ZS), BF)...  40.1 us
    pallas_call x1, Pallas kernels, local(): pl.pallas_call(unpack, out_shape=tuple((jax.ShapeDtypeStruct(s, F32) for...  2.23 us

profile of v2, /device:TPU:1, one launch (start us, length us, event | category | flops | bytes accessed | tf_op | source)
XLA Modules:
  0.0 43.0 jit_solution(11835448206580134473)
XLA Ops:
  0.6 40.1 %backward.1 = (bf16[2,16,64,128]{3,2,1,0:T(8,128)(2,1)}, bf16[2,16,16,128]{3,2,1,0:T(8,128)(2,1)}) custom-call(bf16[1,4,1,8,128]{4,3,2,1,0:T(8,128)(2,1)} %vol_h.1, bf16[1,128,1,8,128]{4,3,2,1,0:T(8,128)(2,1)} %cot.1, bf16[3,3,3,4,32]{4,3,2,1,0:T(4,128)(2,1)} %w1_h.1, f32[32]{0:T(128)} %b1_h.1, bf16[3,3,3,32,64]{4,3,2,1,0:T(8,128)(2,1)} %w2_h.1, f32[64]{0:T(128)} %b2_h.1, ...), custom_call_target="tpu_custom_call" | custom-call | tf_op jit(solution)/shard_map/backward/pallas_call | solution.py:407
  40.8 2.2 %widen.1 = (f32[3,3,3,4,32]{4,3,2,1,0:T(4,128)}, f32[32]{0:T(128)}, f32[3,3,3,32,64]{4,3,2,1,0:T(8,128)}, f32[64]{0:T(128)}, f32[3,3,3,64,128]{4,3,2,1,0:T(8,128)}, /*index=5*/f32[128]{0:T(128)}) custom-call(bf16[2,16,64,128]{3,2,1,0:T(8,128)(2,1)} %get-tuple-element.8.in_a, bf16[2,16,16,128]{3,2,1,0:T(8,128)(2,1)} %get-tuple-element.9.in_b), custom_call_target="tpu_custom_call" | custom-call | tf_op jit(solution)/shard_map/widen/pallas_call | solution.py:434

commit v3 on v2

--- a/solution.py
+++ b/solution.py
@@ -18,17 +18,12 @@
 NT = (((1,), (1,)), ((), ()))
 
 
-def softplus_sigmoid(u):
+def leaky(u):
+    return 0.3 * u + 0.7 * (jnp.maximum(u, 0.0) + jnp.log(1.0 + jnp.exp(-jnp.abs(u))))
+
+
+def slope(u):
     e = jnp.exp(-jnp.abs(u))
-    return jnp.maximum(u, 0.0) + jnp.log(1.0 + e), e
-
-
-def leaky(u):
-    soft, e = softplus_sigmoid(u)
-    return 0.3 * u + 0.7 * soft, e
-
-
-def slope_from(u, e):
     r = 1.0 / (1.0 + e)
     return 0.3 + 0.7 * jnp.where(u >= 0.0, r, e * r)
 
@@ -58,15 +53,15 @@
 
 def body(
     vol_h, cot, w1_h, b1_h, w2_h, b2_h, w3_h, b3_h,
-    out_a, out_b,
-    gath_a, gath_b, outs,
+    out_a, out_b, out_c,
+    gath_a, gath_b, fin, outs,
     vol, w1, b1, w2, b2, w3, b3, ins,
     vols, cotv, cotf, volf, w1f, w1big, w2big, w3t, w3b, w2b, bcols,
-    s1, q1, q2, r3, r2, pre, d3, d2, d1, sl1, sl2, fl,
+    s1, q1, q2, r3, r2, pre1, pre2, pre3, d3, d2, d1, sl1, sl2, fl,
     acc_a, own_a, rx_a0, sum_a, rx_a1, z_a,
     g2, acc_b, rx_b0, sum_b, rx_b1, z_b,
-    g1,
-    vs, vr, a_s, a_r, b_s, b_r, ready,
+    g1, acc_c, rx_c0, x_c, z_c,
+    vs, vr, a_s, a_r, b_s, b_r, c_s, c_r, ready,
 ):
     me_s, me_p = lax.axis_index("sample"), lax.axis_index("space")
     zh, y, c = me_s // 8, (me_s // 2) % 4, me_s % 2
@@ -75,24 +70,42 @@
     zi = zh * 4 + zl
     partner = (me_s + 1 - 2 * c, me_p)
 
-    def xy_peer(d):
-        r = (rank + d) % 16
-        return r, (zh * 8 + (r % 4) * 2 + c, (r // 4) * 4 + zl)
-
-    def z_peer(d):
+    def hops(d, n):
+        return min(d, n - d)
+
+    xy_peers = []
+    for dx, dy in sorted([(i, j) for i in range(4) for j in range(4)], key=lambda o: -hops(o[0], 4) - hops(o[1], 4))[:15]:
+        px, py = (x + dx) % 4, (y + dy) % 4
+        xy_peers.append((px * 4 + py, (zh * 8 + py * 2 + c, px * 4 + zl)))
+    z_peers = []
+    for d in sorted(range(1, 8), key=lambda o: -hops(o, 8)):
         z = (zi + d) % 8
-        return ((z // 4) * 8 + y * 2 + c, x * 4 + z % 4)
+        z_peers.append(((z // 4) * 8 + y * 2 + c, x * 4 + z % 4))
 
     near = [(j, (me_p + j >= 0) & (me_p + j < NX)) for j in (1, -1, 2, -2, 3, -3)]
 
     leaving = []
+
+    def drain():
+        for cond, wait in leaving:
+            if cond is True:
+                wait()
+            else:
+                pl.when(cond)(wait)
+        leaving.clear()
+
+    loads = [
+        pltpu.make_async_copy(src, dst, ins.at[i])
+        for i, (src, dst) in enumerate(((vol_h, vol), (w1_h, w1), (b1_h, b1), (b2_h, b2), (b3_h, b3), (w2_h, w2), (w3_h, w3), (cot, cotv)))
+    ]
+    loads[0].start()
 
     x_line = [(me_s, (me_p + 4 * d) % 16) for d in (2, 1, 3)]
     y_line = [(zh * 8 + ((y + d) % 4) * 2 + c, me_p) for d in (2, 1, 3)]
     z_line = [(me_s, 4 * x + (zl + d) % 4) for d in (1, 2, 3)]
     barrier = pltpu.get_barrier_semaphore()
     count = jnp.int32(8)
-    for j, ok in near[::-1]:
+    for j, ok in near:
         @pl.when(ok)
         def _():
             pl.semaphore_signal(barrier, 1, device_id=(me_s, me_p + j), device_id_type=MESH)
@@ -100,15 +113,8 @@
     for dev in [((me_s + 8) % 16, me_p)] + x_line + y_line + [partner]:
         pl.semaphore_signal(barrier, 1, device_id=dev, device_id_type=MESH)
 
-    loads = [
-        pltpu.make_async_copy(src, dst, ins.at[i])
-        for i, (src, dst) in enumerate(((w1_h, w1), (b1_h, b1), (b2_h, b2), (b3_h, b3), (vol_h, vol), (w2_h, w2), (w3_h, w3), (cot, cotv)))
-    ]
-    for load in loads:
-        load.start()
-
     lane = lax.broadcasted_iota(jnp.int32, (1, ZS), 1)
-    loads[4].wait()
+    loads[0].wait()
     pl.semaphore_wait(barrier, count)
 
 
@@ -119,11 +125,14 @@
         pl.when(ok)(copy.start)
         leaving.append((ok, copy.wait_send))
 
+    for load in loads[1:]:
+        load.start()
+
     for dev in x_line + z_line:
         pl.semaphore_signal(ready, 1, device_id=dev, device_id_type=MESH)
 
     w1f[...] = jnp.zeros_like(w1f)
-    for load in loads[:4]:
+    for load in loads[1:5]:
         load.wait()
     for kx in range(3):
         for ky in range(3):
@@ -144,7 +153,8 @@
     zero_edges(s1, 0, 32)
     for xo in range(5):
         zero_edges(q1, xo * 288, C1)
-    q1[1440:1536, :] = jnp.zeros((96, CELLS), BF)
+    q1[1440:1472, :] = jnp.ones((32, CELLS), BF)
+    q1[1472:1536, :] = jnp.zeros((64, CELLS), BF)
     for xo in range(3):
         zero_edges(q2, xo * 576, C2)
     q2[1728:1744, :] = jnp.ones((16, CELLS), BF)
@@ -196,55 +206,61 @@
     for yy in range(YS):
         spread(s1, 0, volf[pl.ds(yy, 32, stride=YS), :], yy, lane)
 
-    pre[0:160, :] = jnp.dot(w1big[...], s1[...], preferred_element_type=F32)
+    def alive(plane):
+        return jnp.where((plane >= 0) & (plane < NX), 1.0, 0.0).astype(F32)
+
+    def slopes(sl, pre, bias, planes, width):
+        for xo in range(planes):
+            rows = slice(xo * width, (xo + 1) * width)
+            live = alive(me_p + xo - planes // 2)
+            for yy in range(YS):
+                cut = slice(yy * ZS, (yy + 1) * ZS)
+                sl[rows, cut] = slope(pre[rows, cut] + bias) * live
+
+    pre1[...] = jnp.dot(w1big[...], s1[...], preferred_element_type=F32)
     for xo in range(5):
         plane = me_p + xo - 2
-        live = jnp.where((plane >= 0) & (plane < NX), 1.0, 0.0).astype(F32)
+        live = alive(plane)
         for yy in range(YS):
-            u = pre[xo * C1 : (xo + 1) * C1, yy * ZS : (yy + 1) * ZS] + bcols[0:C1, :]
-            a, e = leaky(u)
-            sl1[xo * C1 : (xo + 1) * C1, yy * ZS : (yy + 1) * ZS] = slope_from(u, e) * live
+            u = pre1[xo * C1 : (xo + 1) * C1, yy * ZS : (yy + 1) * ZS] + bcols[0:C1, :]
+            a = leaky(u)
             spread(q1, xo * 288, a * live, yy, lane)
 
-    pre[0:192, :] = jnp.dot(w2big[...], q1[...], preferred_element_type=F32)
+    pre2[...] = jnp.dot(w2big[...], q1[...], preferred_element_type=F32)
     for xo in range(3):
         plane = me_p + xo - 1
-        live = jnp.where((plane >= 0) & (plane < NX), 1.0, 0.0).astype(F32)
+        live = alive(plane)
         for yy in range(YS):
-            u = pre[xo * C2 : (xo + 1) * C2, yy * ZS : (yy + 1) * ZS] + bcols[C2 : 2 * C2, :]
-            a, e = leaky(u)
-            sl2[xo * C2 : (xo + 1) * C2, yy * ZS : (yy + 1) * ZS] = slope_from(u, e) * live
+            u = pre2[xo * C2 : (xo + 1) * C2, yy * ZS : (yy + 1) * ZS] + bcols[C2 : 2 * C2, :]
+            a = leaky(u)
             spread(q2, xo * 576, a * live, yy, lane)
 
-    pre[0:C3, :] = jnp.dot(w3t[...], q2[0:1792, :], preferred_element_type=F32)
+    pre3[...] = jnp.dot(w3t[...], q2[0:1792, :], preferred_element_type=F32)
     for yy in range(YS):
-        u = pre[0:C3, yy * ZS : (yy + 1) * ZS] + b3col
-        e = jnp.exp(-jnp.abs(u))
-        delta = cotf[pl.ds(yy, C3, stride=YS), :] * SCALE * slope_from(u, e)
+        u = pre3[:, yy * ZS : (yy + 1) * ZS] + b3col
+        delta = cotf[pl.ds(yy, C3, stride=YS), :] * SCALE * slope(u)
         d3[:, yy * ZS : (yy + 1) * ZS] = delta.astype(BF)
         spread(r3, 0, delta, yy, lane)
 
     def xy_scatter(total, rx, send_sem, recv_sem):
-        for d in range(1, 16):
-            r, dev = xy_peer(d)
+        for n, (r, dev) in enumerate(xy_peers):
             pltpu.make_async_remote_copy(
-                src_ref=total.at[r], dst_ref=rx.at[d - 1], send_sem=send_sem, recv_sem=recv_sem,
+                src_ref=total.at[r], dst_ref=rx.at[n], send_sem=send_sem, recv_sem=recv_sem,
                 device_id=dev, device_id_type=MESH).start()
         leaving.append((True, lambda: wait_bytes(rx, send_sem)))
 
     def xy_gather(buf, send_sem, recv_sem):
-        for d in range(1, 16):
-            _, dev = xy_peer(d)
+        for _, dev in xy_peers:
             pltpu.make_async_remote_copy(
                 src_ref=buf.at[rank], dst_ref=buf.at[rank], send_sem=send_sem, recv_sem=recv_sem,
                 device_id=dev, device_id_type=MESH).start()
         leaving.append((True, lambda: wait_bytes(buf.at[pl.ds(0, 15)], send_sem)))
 
     def z_gather(buf, send_sem, recv_sem):
-        for d in range(1, 8):
+        for dev in z_peers:
             pltpu.make_async_remote_copy(
                 src_ref=buf.at[zi], dst_ref=buf.at[zi], send_sem=send_sem, recv_sem=recv_sem,
-                device_id=z_peer(d), device_id_type=MESH).start()
+                device_id=dev, device_id_type=MESH).start()
         leaving.append((True, lambda: wait_bytes(buf.at[pl.ds(0, 7)], send_sem)))
 
     def wait_bytes(ref, sem):
@@ -267,6 +283,8 @@
 
     own_a[...] = lax.dot_general(q2[pl.ds(mine, 1024), :], d3[...], NT, preferred_element_type=F32)
 
+    slopes(sl2, pre2, bcols[C2 : 2 * C2, :], 3, C2)
+
     fl[...] = jnp.dot(w3b[...], r3[...], preferred_element_type=F32)
 
     copy_a0.wait_recv()
@@ -281,10 +299,7 @@
             d2[rows, cut] = delta.astype(BF)
             spread(r2, xo * 576, delta, yy, lane)
 
-    d1[...] = (jnp.dot(w2b[...], r2[...], preferred_element_type=F32) * sl1[...]).astype(BF)
-
-    g2[0:1440, :] = lax.dot_general(q1[0:1440, :], d2[...], NT, preferred_element_type=F32)
-    g2[1440:1472, :] = lax.dot_general(s1[288:320, :], d2[...], NT, preferred_element_type=F32)
+    g2[...] = lax.dot_general(q1[0:1472, :], d2[...], NT, preferred_element_type=F32)
 
     def tap_two(n):
         if n == 27:
@@ -296,8 +311,23 @@
         acc_b[0, i] = rows[0:16].astype(BF)
         acc_b[1, i] = rows[16:32].astype(BF)
 
+    for i in (14, 15):
+        pack_b(i, jnp.zeros((32, ZS), F32))
     for i in range(14):
         pack_b(i, jnp.concatenate([tap_two(2 * i), tap_two(2 * i + 1)], axis=1))
+
+    copy_b0 = pltpu.make_async_remote_copy(
+        src_ref=acc_b.at[1 - c], dst_ref=rx_b0, send_sem=b_s.at[0], recv_sem=b_r.at[0], device_id=partner, device_id_type=MESH)
+    copy_b0.start()
+    leaving.append((True, copy_b0.wait_send))
+
+    slopes(sl1, pre1, bcols[0:C1, :], 5, C1)
+
+    d1[...] = (jnp.dot(w2b[...], r2[...], preferred_element_type=F32) * sl1[...]).astype(BF)
+
+    copy_b0.wait_recv()
+    sum_b[...] = (acc_b[c].astype(F32) + rx_b0[...].astype(F32)).astype(BF)
+    xy_scatter(sum_b, rx_b1, b_s.at[1], b_r.at[1])
 
     g1[...] = lax.dot_general(s1[0:320, :], d1[...], NT, preferred_element_type=F32)
 
@@ -308,16 +338,15 @@
             return sum(g1[288:304, p * C1 : (p + 1) * C1] for p in range(5))
         return sum(g1[b * 32 + 4 * p : b * 32 + 4 * p + 16, p * C1 : (p + 1) * C1] for p in range(5))
 
-    rows_one = [jnp.concatenate([tap_one(4 * g + i) for i in range(4)], axis=1) for g in range(3)]
-    pack_b(14, jnp.concatenate(rows_one[0:2], axis=0))
-    pack_b(15, jnp.concatenate([rows_one[2], jnp.zeros((16, ZS), F32)], axis=0))
-    copy_b0 = pltpu.make_async_remote_copy(
-        src_ref=acc_b.at[1 - c], dst_ref=rx_b0, send_sem=b_s.at[0], recv_sem=b_r.at[0], device_id=partner, device_id_type=MESH)
-    copy_b0.start()
-    leaving.append((True, copy_b0.wait_send))
-    copy_b0.wait_recv()
-    sum_b[...] = (acc_b[c].astype(F32) + rx_b0[...].astype(F32)).astype(BF)
-    xy_scatter(sum_b, rx_b1, b_s.at[1], b_r.at[1])
+    for g in range(3):
+        acc_c[g * 16 : (g + 1) * 16, :] = jnp.concatenate([tap_one(4 * g + i) for i in range(4)], axis=1).astype(BF)
+    copy_c0 = pltpu.make_async_remote_copy(
+        src_ref=acc_c, dst_ref=rx_c0, send_sem=c_s.at[0], recv_sem=c_r.at[0], device_id=partner, device_id_type=MESH)
+    copy_c0.start()
+    leaving.append((True, copy_c0.wait_send))
+    copy_c0.wait_recv()
+    x_c[rank] = (acc_c[...].astype(F32) + rx_c0[...].astype(F32)).astype(BF)
+    xy_gather(x_c, c_s.at[1], c_r.at[1])
 
     wait_bytes(rx_a1, a_r.at[1])
     z_a[zi] = (sum_a[rank].astype(F32) + total_of(rx_a1, 15)).astype(BF)
@@ -329,6 +358,9 @@
     half = gath_a.at[c]
     half[rank] = total_of(z_a, 8).astype(BF)
     xy_gather(half, a_s.at[3], a_r.at[3])
+    wait_bytes(x_c.at[pl.ds(0, 15)], c_r.at[1])
+    z_c[zi] = total_of(x_c, 16).astype(BF)
+    z_gather(z_c, c_s.at[2], c_r.at[2])
     wait_bytes(z_b.at[pl.ds(0, 7)], b_r.at[2])
     half_b = gath_b.at[c]
     half_b[rank] = total_of(z_b, 8).astype(BF)
@@ -339,64 +371,68 @@
         copy.start()
         leaving.append((True, copy.wait))
 
+    drain()
+
+    wait_bytes(z_c.at[pl.ds(0, 7)], c_r.at[2])
+    fin[...] = total_of(z_c, 8)
+    write(0, fin, out_c)
+
+    def to_partner(i, src, dst, send_sem, recv_sem):
+        copy = pltpu.make_async_remote_copy(
+            src_ref=src, dst_ref=dst, send_sem=send_sem, recv_sem=recv_sem, device_id=partner, device_id_type=MESH)
+        copy.start()
+        write(i, src, dst)
+        leaving.append((True, copy.wait))
+
     wait_bytes(half.at[pl.ds(0, 15)], a_r.at[3])
-    copy_a4 = pltpu.make_async_remote_copy(
-        src_ref=half, dst_ref=half, send_sem=a_s.at[4], recv_sem=a_r.at[4], device_id=partner, device_id_type=MESH)
-    copy_a4.start()
-    leaving.append((True, copy_a4.wait_send))
-    write(1, half, out_a.at[c])
-
+    to_partner(1, half, out_a.at[c], a_s.at[4], a_r.at[4])
     wait_bytes(half_b.at[pl.ds(0, 15)], b_r.at[3])
-    copy_b4 = pltpu.make_async_remote_copy(
-        src_ref=half_b, dst_ref=half_b, send_sem=b_s.at[4], recv_sem=b_r.at[4], device_id=partner, device_id_type=MESH)
-    copy_b4.start()
-    leaving.append((True, copy_b4.wait_send))
-    copy_a4.wait_recv()
-    write(2, gath_a.at[1 - c], out_a.at[1 - c])
-    copy_b4.wait_recv()
-    write(0, gath_b, out_b)
-
-    for cond, wait in leaving:
-        if cond is True:
-            wait()
-        else:
-            pl.when(cond)(wait)
-
-
-def unpack(in_a, in_b, o1, ob1, o2, ob2, o3, ob3, gath_a, gath_b, v1, vb1, v2, vb2, v3, vb3, sems, ins):
-    pairs = ((in_a.at[0], gath_a.at[0]), (in_a.at[1], gath_a.at[1]), (in_b, gath_b))
+    to_partner(2, half_b, out_b.at[c], b_s.at[4], b_r.at[4])
+
+    drain()
+
+
+def unpack(in_a, in_b, in_c, o1, ob1, o2, ob2, o3, ob3, gath_a, gath_b, fin, v1, vb1, v2, vb2, v3, vb3, sems, ins):
+    pairs = ((in_a.at[0], gath_a.at[0]), (in_a.at[1], gath_a.at[1]), (in_b, gath_b), (in_c, fin))
     loads = [pltpu.make_async_copy(src, dst, ins.at[i]) for i, (src, dst) in enumerate(pairs)]
     for load in loads:
         load.start()
-    outs = (o3, o2, o1, ob1, ob2, ob3)
-    copies = [pltpu.make_async_copy(v, o, sems.at[i]) for i, (v, o) in enumerate(zip((v3, v2, v1, vb1, vb2, vb3), outs))]
-    loads[0].wait()
-    loads[1].wait()
-    for t in range(27):
-        v3[t // 9, (t // 3) % 3, t % 3] = gath_a[t // 16, t % 16].astype(F32)
-    copies[0].start()
-    loads[2].wait()
+    started = []
+
+    def write(src, dst):
+        copy = pltpu.make_async_copy(src, dst, sems.at[len(started)])
+        copy.start()
+        started.append(copy)
 
     def rows_b(i):
         return jnp.concatenate([gath_b[0, i].astype(F32), gath_b[1, i].astype(F32)], axis=0)
 
+    for kx in range(3):
+        if kx == 0:
+            loads[0].wait()
+        for t in range(9 * kx, 9 * kx + 9):
+            if t == 16:
+                loads[1].wait()
+            v3[t // 9, (t // 3) % 3, t % 3] = gath_a[t // 16, t % 16].astype(F32)
+        write(v3.at[kx], o3.at[kx])
+    vb3[...] = gath_a[1, 11].astype(F32)[0:1, :].reshape(C3)
+    write(vb3, ob3)
+    loads[2].wait()
     for t in range(27):
         i, s = t // 2, (t % 2) * 64
         v2[t // 9, (t // 3) % 3, t % 3] = rows_b(i)[:, s : s + 64]
-    copies[1].start()
-    fin = jnp.concatenate([rows_b(14), rows_b(15)], axis=0)
+    write(v2, o2)
+    vb2[...] = rows_b(13)[0:1, 64:128].reshape(C2)
+    write(vb2, ob2)
+    loads[3].wait()
     for b in range(9):
         g, i = b // 4, b % 4
         for kx in range(3):
             v1[kx, b // 3, b % 3] = fin[g * 16 + kx * 4 : g * 16 + kx * 4 + 4, i * 32 : i * 32 + 32]
-    copies[2].start()
+    write(v1, o1)
     vb1[...] = fin[32:33, 32:64].reshape(C1)
-    copies[3].start()
-    vb2[...] = rows_b(13)[0:1, 64:128].reshape(C2)
-    copies[4].start()
-    vb3[...] = gath_a[1, 11].astype(F32)[0:1, :].reshape(C3)
-    copies[5].start()
-    for copy in copies:
+    write(vb1, ob1)
+    for copy in started:
         copy.wait()
 
 
@@ -409,23 +445,24 @@
         out_shape=(
             jax.ShapeDtypeStruct((2, 16, 64, ZS), BF),
             jax.ShapeDtypeStruct((2, 16, 16, ZS), BF),
+            jax.ShapeDtypeStruct((48, ZS), F32),
         ),
         in_specs=[hbm] * 8,
-        out_specs=(hbm,) * 2,
+        out_specs=(hbm,) * 3,
         scratch_shapes=[
-            V((2, 16, 64, ZS), BF), V((2, 16, 16, ZS), BF), D((3,)),
+            V((2, 16, 64, ZS), BF), V((2, 16, 16, ZS), BF), V((48, ZS), F32), D((3,)),
             V((1, C0, 1, YS, ZS), BF), V((3, 3, 3, C0, C1), BF), V((C1,), F32), V((3, 3, 3, C1, C2), BF), V((C2,), F32),
             V((3, 3, 3, C2, C3), BF), V((C3,), F32), D((8,)),
             V((7, C0, YS, ZS), BF), V((1, C3, 1, YS, ZS), BF), V((C3 * YS, ZS), F32), V((256, ZS), F32),
             V((384, ZS), F32), V((160, 384), BF), V((192, 1536), BF), V((C3, 1792), BF), V((192, 1152), BF), V((160, 1792), BF),
             V((ZS, ZS), F32),
             V((384, CELLS), BF), V((1536, CELLS), BF), V((2048, CELLS), BF), V((1152, CELLS), BF), V((1792, CELLS), BF),
-            V((192, CELLS), F32), V((C3, CELLS), BF), V((192, CELLS), BF), V((160, CELLS), BF), V((160, CELLS), F32), V((192, CELLS), F32),
+            V((160, CELLS), F32), V((192, CELLS), F32), V((C3, CELLS), F32), V((C3, CELLS), BF), V((192, CELLS), BF), V((160, CELLS), BF), V((160, CELLS), F32), V((192, CELLS), F32),
             V((192, CELLS), F32),
             V((1024, ZS), BF), V((1024, ZS), F32), V((1024, ZS), BF), V((16, 64, ZS), BF), V((15, 64, ZS), BF), V((8, 64, ZS), BF),
             V((1472, 192), F32), V((2, 16, 16, ZS), BF), V((16, 16, ZS), BF), V((16, 16, ZS), BF), V((15, 16, ZS), BF), V((8, 16, ZS), BF),
-            V((320, 160), F32),
-            D((7,)), D((7,)), D((5,)), D((5,)), D((5,)), D((5,)), pltpu.SemaphoreType.REGULAR,
+            V((320, 160), F32), V((48, ZS), BF), V((48, ZS), BF), V((16, 48, ZS), BF), V((8, 48, ZS), BF),
+            D((7,)), D((7,)), D((5,)), D((5,)), D((5,)), D((5,)), D((3,)), D((3,)), pltpu.SemaphoreType.REGULAR,
         ],
         compiler_params=pltpu.CompilerParams(collective_id=0, has_side_effects=True, vmem_limit_bytes=62 << 20),
         name="backward",
@@ -434,11 +471,11 @@
     return pl.pallas_call(
         unpack,
         out_shape=tuple(jax.ShapeDtypeStruct(s, F32) for s in shapes),
-        in_specs=[hbm] * 2,
+        in_specs=[hbm] * 3,
         out_specs=(hbm,) * 6,
-        scratch_shapes=[V((2, 16, 64, ZS), BF), V((2, 16, 16, ZS), BF)]
+        scratch_shapes=[V((2, 16, 64, ZS), BF), V((2, 16, 16, ZS), BF), V((48, ZS), F32)]
         + [V(s, F32) for s in shapes]
-        + [D((6,)), D((3,))],
+        + [D((8,)), D((4,))],
         compiler_params=pltpu.CompilerParams(vmem_limit_bytes=62 << 20),
         name="widen",
     )(*sums)

time: 43.1 us -> 42.9 us (level)
  no operation moved by 1% of the time
where the time goes in v3:
time: 42.9 us; the launch traced here: 42.7 us
  Pallas kernels  42.1 us (98%)
  between operations  0.64 us (1%)
    pallas_call x1, Pallas kernels, local(): pl.pallas_call(body, out_shape=(jax.ShapeDtypeStruct((2, 16, 64, ZS), BF)...  39.9 us
    pallas_call x1, Pallas kernels, local(): pl.pallas_call(unpack, out_shape=tuple((jax.ShapeDtypeStruct(s, F32) for...  2.15 us

profile of v3, /device:TPU:1, one launch (start us, length us, event | category | flops | bytes accessed | tf_op | source)
XLA Modules:
  0.0 42.7 jit_solution(10142453200027293814)
XLA Ops:
  0.6 39.9 %backward.1 = (bf16[2,16,64,128]{3,2,1,0:T(8,128)(2,1)}, bf16[2,16,16,128]{3,2,1,0:T(8,128)(2,1)}, f32[48,128]{1,0:T(8,128)}) custom-call(bf16[1,4,1,8,128]{4,3,2,1,0:T(8,128)(2,1)} %vol_h.1, bf16[1,128,1,8,128]{4,3,2,1,0:T(8,128)(2,1)} %cot.1, bf16[3,3,3,4,32]{4,3,2,1,0:T(4,128)(2,1)} %w1_h.1, f32[32]{0:T(128)} %b1_h.1, bf16[3,3,3,32,64]{4,3,2,1,0:T(8,128)(2,1)} %w2_h.1, ...), custom_call_target="tpu_custom_call" | custom-call | tf_op jit(solution)/shard_map/backward/pallas_call | solution.py:443
  40.6 2.1 %widen.1 = (f32[3,3,3,4,32]{4,3,2,1,0:T(4,128)}, f32[32]{0:T(128)}, f32[3,3,3,32,64]{4,3,2,1,0:T(8,128)}, f32[64]{0:T(128)}, f32[3,3,3,64,128]{4,3,2,1,0:T(8,128)}, /*index=5*/f32[128]{0:T(128)}) custom-call(bf16[2,16,64,128]{3,2,1,0:T(8,128)(2,1)} %get-tuple-element.9.in_a, bf16[2,16,16,128]{3,2,1,0:T(8,128)(2,1)} %get-tuple-element.10.in_b, ...), custom_call_target="tpu_custom_call" | custom-call | tf_op jit(solution)/shard_map/widen/pallas_call | solution.py:471

commit v4 on v3

--- a/solution.py
+++ b/solution.py
@@ -272,24 +272,32 @@
             t = t + ref[i].astype(F32)
         return t
 
-    other = pl.multiple_of((1 - c) * 1024, 1024)
-    mine = pl.multiple_of(c * 1024, 1024)
-    acc_a[...] = lax.dot_general(q2[pl.ds(other, 1024), :], d3[...], NT, preferred_element_type=F32).astype(BF)
+    other = pl.multiple_of((1 - c) * 896, 896)
+    mine = pl.multiple_of(c * 896, 896)
+    acc_a[...] = lax.dot_general(q2[pl.ds(other, 896), :], d3[...], NT, preferred_element_type=F32).astype(BF)
     copy_a0 = pltpu.make_async_remote_copy(
         src_ref=acc_a, dst_ref=rx_a0, send_sem=a_s.at[0], recv_sem=a_r.at[0],
         device_id=partner, device_id_type=MESH)
     copy_a0.start()
     leaving.append((True, copy_a0.wait_send))
 
-    own_a[...] = lax.dot_general(q2[pl.ds(mine, 1024), :], d3[...], NT, preferred_element_type=F32)
+    own_a[...] = lax.dot_general(q2[pl.ds(mine, 896), :], d3[...], NT, preferred_element_type=F32)
 
     slopes(sl2, pre2, bcols[C2 : 2 * C2, :], 3, C2)
 
     fl[...] = jnp.dot(w3b[...], r3[...], preferred_element_type=F32)
 
     copy_a0.wait_recv()
-    sum_a[...] = (own_a[...] + rx_a0[...].astype(F32)).astype(BF).reshape(16, 64, ZS)
-    xy_scatter(sum_a, rx_a1, a_s.at[1], a_r.at[1])
+    sum_a[...] = (own_a[...] + rx_a0[...].astype(F32)).astype(BF).reshape(14, 64, ZS)
+    for n, (r, dev) in enumerate(xy_peers):
+        chunk = r - (r // 14) * (r - 13)
+        copy = pltpu.make_async_remote_copy(
+            src_ref=sum_a.at[chunk], dst_ref=rx_a1.at[n], send_sem=a_s.at[1], recv_sem=a_r.at[1],
+            device_id=dev, device_id_type=MESH)
+        pl.when(r < 14)(copy.start)
+    owner, idle = rank < 14, rank >= 14
+    leaving.append((owner, lambda: wait_bytes(rx_a1.at[pl.ds(0, 13)], a_s.at[1])))
+    leaving.append((idle, lambda: wait_bytes(rx_a1.at[pl.ds(0, 14)], a_s.at[1])))
 
     for xo in range(3):
         rows = slice(xo * C2, (xo + 1) * C2)
@@ -348,16 +356,25 @@
     x_c[rank] = (acc_c[...].astype(F32) + rx_c0[...].astype(F32)).astype(BF)
     xy_gather(x_c, c_s.at[1], c_r.at[1])
 
-    wait_bytes(rx_a1, a_r.at[1])
-    z_a[zi] = (sum_a[rank].astype(F32) + total_of(rx_a1, 15)).astype(BF)
-    z_gather(z_a, a_s.at[2], a_r.at[2])
+    @pl.when(owner)
+    def _():
+        wait_bytes(rx_a1, a_r.at[1])
+        z_a[zi] = (sum_a[rank - (rank // 14) * (rank - 13)].astype(F32) + total_of(rx_a1, 15)).astype(BF)
+        z_gather(z_a, a_s.at[2], a_r.at[2])
+
+    leaving[-1] = (owner, lambda: wait_bytes(z_a.at[pl.ds(0, 7)], a_s.at[2]))
     wait_bytes(rx_b1, b_r.at[1])
     z_b[zi] = (sum_b[rank].astype(F32) + total_of(rx_b1, 15)).astype(BF)
     z_gather(z_b, b_s.at[2], b_r.at[2])
-    wait_bytes(z_a.at[pl.ds(0, 7)], a_r.at[2])
     half = gath_a.at[c]
-    half[rank] = total_of(z_a, 8).astype(BF)
-    xy_gather(half, a_s.at[3], a_r.at[3])
+
+    @pl.when(owner)
+    def _():
+        wait_bytes(z_a.at[pl.ds(0, 7)], a_r.at[2])
+        half[rank] = total_of(z_a, 8).astype(BF)
+        xy_gather(half, a_s.at[3], a_r.at[3])
+
+    leaving[-1] = (owner, lambda: wait_bytes(gath_a.at[c, pl.ds(0, 15)], a_s.at[3]))
     wait_bytes(x_c.at[pl.ds(0, 15)], c_r.at[1])
     z_c[zi] = total_of(x_c, 16).astype(BF)
     z_gather(z_c, c_s.at[2], c_r.at[2])
@@ -384,8 +401,9 @@
         write(i, src, dst)
         leaving.append((True, copy.wait))
 
-    wait_bytes(half.at[pl.ds(0, 15)], a_r.at[3])
-    to_partner(1, half, out_a.at[c], a_s.at[4], a_r.at[4])
+    pl.when(owner)(lambda: wait_bytes(half.at[pl.ds(0, 13)], a_r.at[3]))
+    pl.when(idle)(lambda: wait_bytes(half.at[pl.ds(0, 14)], a_r.at[3]))
+    to_partner(1, half.at[pl.ds(0, 14)], out_a.at[c, pl.ds(0, 14)], a_s.at[4], a_r.at[4])
     wait_bytes(half_b.at[pl.ds(0, 15)], b_r.at[3])
     to_partner(2, half_b, out_b.at[c], b_s.at[4], b_r.at[4])
 
@@ -411,11 +429,11 @@
         if kx == 0:
             loads[0].wait()
         for t in range(9 * kx, 9 * kx + 9):
-            if t == 16:
+            if t == 14:
                 loads[1].wait()
-            v3[t // 9, (t // 3) % 3, t % 3] = gath_a[t // 16, t % 16].astype(F32)
+            v3[t // 9, (t // 3) % 3, t % 3] = gath_a[t // 14, t % 14].astype(F32)
         write(v3.at[kx], o3.at[kx])
-    vb3[...] = gath_a[1, 11].astype(F32)[0:1, :].reshape(C3)
+    vb3[...] = gath_a[1, 13].astype(F32)[0:1, :].reshape(C3)
     write(vb3, ob3)
     loads[2].wait()
     for t in range(27):
@@ -459,7 +477,7 @@
             V((384, CELLS), BF), V((1536, CELLS), BF), V((2048, CELLS), BF), V((1152, CELLS), BF), V((1792, CELLS), BF),
             V((160, CELLS), F32), V((192, CELLS), F32), V((C3, CELLS), F32), V((C3, CELLS), BF), V((192, CELLS), BF), V((160, CELLS), BF), V((160, CELLS), F32), V((192, CELLS), F32),
             V((192, CELLS), F32),
-            V((1024, ZS), BF), V((1024, ZS), F32), V((1024, ZS), BF), V((16, 64, ZS), BF), V((15, 64, ZS), BF), V((8, 64, ZS), BF),
+            V((896, ZS), BF), V((896, ZS), F32), V((896, ZS), BF), V((14, 64, ZS), BF), V((15, 64, ZS), BF), V((8, 64, ZS), BF),
             V((1472, 192), F32), V((2, 16, 16, ZS), BF), V((16, 16, ZS), BF), V((16, 16, ZS), BF), V((15, 16, ZS), BF), V((8, 16, ZS), BF),
             V((320, 160), F32), V((48, ZS), BF), V((48, ZS), BF), V((16, 48, ZS), BF), V((8, 48, ZS), BF),
             D((7,)), D((7,)), D((5,)), D((5,)), D((5,)), D((5,)), D((3,)), D((3,)), pltpu.SemaphoreType.REGULAR,

time: 42.9 us -> 42.7 us (level)
  no operation moved by 1% of the time
where the time goes in v4:
time: 42.7 us; the launch traced here: 42.5 us
  Pallas kernels  41.9 us (98%)
  between operations  0.64 us (1%)
    pallas_call x1, Pallas kernels, local(): pl.pallas_call(body, out_shape=(jax.ShapeDtypeStruct((2, 16, 64, ZS), BF)...  39.7 us
    pallas_call x1, Pallas kernels, local(): pl.pallas_call(unpack, out_shape=tuple((jax.ShapeDtypeStruct(s, F32) for...  2.15 us

profile of v4, /device:TPU:1, one launch (start us, length us, event | category | flops | bytes accessed | tf_op | source)
XLA Modules:
  0.0 42.5 jit_solution(16996786149555117692)
XLA Ops:
  0.6 39.7 %backward.1 = (bf16[2,16,64,128]{3,2,1,0:T(8,128)(2,1)}, bf16[2,16,16,128]{3,2,1,0:T(8,128)(2,1)}, f32[48,128]{1,0:T(8,128)}) custom-call(bf16[1,4,1,8,128]{4,3,2,1,0:T(8,128)(2,1)} %vol_h.1, bf16[1,128,1,8,128]{4,3,2,1,0:T(8,128)(2,1)} %cot.1, bf16[3,3,3,4,32]{4,3,2,1,0:T(4,128)(2,1)} %w1_h.1, f32[32]{0:T(128)} %b1_h.1, bf16[3,3,3,32,64]{4,3,2,1,0:T(8,128)(2,1)} %w2_h.1, ...), custom_call_target="tpu_custom_call" | custom-call | tf_op jit(solution)/shard_map/backward/pallas_call | solution.py:461
  40.4 2.1 %widen.1 = (f32[3,3,3,4,32]{4,3,2,1,0:T(4,128)}, f32[32]{0:T(128)}, f32[3,3,3,32,64]{4,3,2,1,0:T(8,128)}, f32[64]{0:T(128)}, f32[3,3,3,64,128]{4,3,2,1,0:T(8,128)}, /*index=5*/f32[128]{0:T(128)}) custom-call(bf16[2,16,64,128]{3,2,1,0:T(8,128)(2,1)} %get-tuple-element.9.in_a, bf16[2,16,16,128]{3,2,1,0:T(8,128)(2,1)} %get-tuple-element.10.in_b, ...), custom_call_target="tpu_custom_call" | custom-call | tf_op jit(solution)/shard_map/widen/pallas_call | solution.py:489
